TPU v7x, 512 devices: a whole 4x8x8 slice. The times are simulated.
512 devices in a mesh: grp: 16 (over y, core), sp: 32 (over x, z).
Axes of the slice: x: 4, y: 8, z: 8, core: 2. Of those that a mesh axis runs over, the one named last changes fastest.
Arguments:
- coarse_latent: bfloat16 [16, 32, 16, 512], P(None, 'sp', 'grp'), may hold values from -6 to 6
- renoise: bfloat16 [8192, 2048], P(('grp', 'sp')), may hold values from -6 to 6
- clip_frames: int32 [16, 4], P('grp'), may hold values from 1 to 16, 32 in all within a row
- patch_embed: bfloat16 [64, 1536], replicated, may hold values from -0.75 to 0.75
- mod_shift: float32 [16, 1536], P('grp'), may hold values from -3 to 3
- mod_scale: float32 [16, 1536], P('grp'), may hold values from 0.25 to 1.75
- qkv_weight: bfloat16 [1536, 2304], P(('grp', 'sp')), may hold values from -0.15625 to 0.15625
- out_weight: bfloat16 [1536, 768], P(('grp', 'sp')), may hold values from -1.75 to 1.75
- q_gain: float32 [768], replicated, may hold values from 0.5 to 18
- k_gain: float32 [768], replicated, may hold values from 0.5 to 18
Outputs:
- updated: bfloat16 [262144, 1536], P(('grp', 'sp'))
All inputs are finite; a program needn't handle non-finite values.
Results may differ from a plain program's by a relative error of at most 0.034.
Values may be sent and summed in bfloat16 or wider, within the bound.
A program may use at most 64 MiB of HBM per device.

v0:
```python
import math

import jax
import jax.numpy as jnp
from jax import lax
from jax.sharding import PartitionSpec as P

HEADS = 12
HEAD = 64
C = 16
FH = 16
FW = 32


signal_coef = 0.8
noise_coef = 0.6
epsilon = 1e-06


def head_norm(flat_rows, gains):
    shaped = flat_rows.reshape(flat_rows.shape[0], HEADS, HEAD)
    inverse = lax.rsqrt(jnp.mean(shaped * shaped, axis=2, keepdims=True) + epsilon)
    return (shaped * inverse * gains.reshape(1, HEADS, HEAD)).reshape(
        flat_rows.shape[0], HEADS * HEAD
    )


def local(
    coarse_latent,
    renoise,
    clip_frames,
    patch_embed,
    mod_shift,
    mod_scale,
    qkv_weight,
    out_weight,
    q_gain,
    k_gain,
):
    frames = lax.axis_size("sp")
    width = HEADS * HEAD
    frame_tokens = FH * FW
    per_block = frame_tokens // frames
    local_rows = lax.all_to_all(coarse_latent, "grp", split_axis=0, concat_axis=2, tiled=True)
    pixels = local_rows.reshape(FH, FW, 1, C).astype(jnp.float32)
    upsampled = jnp.broadcast_to(pixels, (FH, FW, 4, C)).reshape(frame_tokens, 4 * C)
    noise_rows = renoise.reshape(frame_tokens, 4 * C).astype(jnp.float32)
    patches = (signal_coef * upsampled + noise_coef * noise_rows).astype(jnp.bfloat16)
    hidden = jnp.dot(patches, patch_embed, preferred_element_type=jnp.float32).astype(jnp.bfloat16)
    hidden_f = hidden.astype(jnp.float32)
    row_mean = jnp.mean(hidden_f, axis=1, keepdims=True)
    centered = hidden_f - row_mean
    row_var = jnp.mean(centered * centered, axis=1, keepdims=True)
    normed = (centered * lax.rsqrt(row_var + epsilon) * mod_scale + mod_shift).astype(jnp.bfloat16)
    qkv_full, out_full = (
        lax.all_gather(qkv_weight, ("grp", "sp"), axis=0, tiled=True),
        lax.all_gather(out_weight, ("grp", "sp"), axis=0, tiled=True),
    )
    counts = clip_frames[0]
    ends = jnp.cumsum(counts)
    positions = jnp.arange(frames, dtype=jnp.int32)
    segment = jnp.sum((positions[:, None] >= ends[None, :]).astype(jnp.int32), axis=1)
    same_clip = segment[:, None] == segment[None, :]
    qkv = jnp.dot(normed, qkv_full, preferred_element_type=jnp.float32)
    query = head_norm(qkv[:, :width], q_gain).astype(jnp.bfloat16)
    keys_all = head_norm(qkv[:, width : 2 * width], k_gain).astype(jnp.bfloat16)
    values_all = qkv[:, 2 * width :].astype(jnp.bfloat16)
    query, keys_all, values_all = (query, keys_all, values_all)
    attend_query = lax.all_to_all(
        query.reshape(1, frames, per_block, width), "sp", split_axis=1, concat_axis=0, tiled=True
    )
    attend_keys_all = lax.all_to_all(
        keys_all.reshape(1, frames, per_block, width), "sp", split_axis=1, concat_axis=0, tiled=True
    )
    attend_values_all = lax.all_to_all(
        values_all.reshape(1, frames, per_block, width),
        "sp",
        split_axis=1,
        concat_axis=0,
        tiled=True,
    )
    count = attend_query.shape[2]
    q_four = attend_query.reshape(frames, count, HEADS, HEAD)
    k_four = attend_keys_all.reshape(frames, count, HEADS, HEAD)
    v_four = attend_values_all.reshape(frames, count, HEADS, HEAD)
    scores = jnp.einsum(
        "fphd,gphd->phfg", q_four, k_four, preferred_element_type=jnp.float32
    ) / math.sqrt(HEAD)
    scores = jnp.where(same_clip[None, None], scores, -jnp.inf)
    top = jnp.max(scores, axis=3, keepdims=True)
    expo = jnp.exp(scores - top)
    probs = (expo / jnp.sum(expo, axis=3, keepdims=True)).astype(jnp.bfloat16)
    mixed = jnp.einsum("phfg,gphd->fphd", probs, v_four, preferred_element_type=jnp.float32).astype(
        jnp.bfloat16
    )
    mixed = lax.all_to_all(
        mixed.reshape(frames, 1, count, width), "sp", split_axis=0, concat_axis=1, tiled=True
    )
    mixed_rows = mixed.reshape(frame_tokens, width)
    attn = lax.dot_general(
        mixed_rows, out_full, (((1,), (1,)), ((), ())), preferred_element_type=jnp.float32
    )
    return (hidden_f + attn).astype(jnp.bfloat16)


def solution(mesh):
    placed = (
        P(None, "sp", "grp", None),
        P(("grp", "sp"), None),
        P("grp", None),
        P(),
        P("grp", None),
        P("grp", None),
        P(("grp", "sp"), None),
        P(("grp", "sp"), None),
        P(),
        P(),
    )
    return jax.shard_map(
        local, mesh=mesh, in_specs=placed, out_specs=P(("grp", "sp"), None), check_vma=False
    )
```

profile of v0, /device:TPU:1, one launch (start us, length us, event | category | flops | bytes accessed | tf_op | source)
XLA Modules:
  0.0 361.7 jit_solution(4672502206222863808)
XLA Ops:
  6.5 0.7 all-gather.5.cloned.1.call-update
  7.8 1.4 reduce.4
  9.8 10.2 %all-to-all-start = ((bf16[16,2,256]{2,1,0:T(2,128)(2,1)}), bf16[16,2,256]{2,1,0:T(2,128)(2,1)S(1)}, u32[]{:S(2)}, u32[]{:S(2)}) async-start(bf16[16,2,256]{2,1,0:T(2,128)(2,1)} %reshape.176), calls=%async_computation | async-start | bytes 32768 | tf_op jit(solution)/shard_map/all_to_all | solution.py:44
  19.9 0.9 convert_multiply_fusion
  21.0 0.7 reduce.2
  21.7 0.7 reduce.1
  22.4 4.9 %all-to-all-done = bf16[16,2,256]{2,1,0:T(2,128)(2,1)S(1)} async-done(((bf16[16,2,256]{2,1,0:T(2,128)(2,1)}), bf16[16,2,256]{2,1,0:T(2,128)(2,1)S(1)}, u32[]{:S(2)}, u32[]{:S(2)}) %all-to-all-start) | async-done | bytes 16416 | tf_op jit(solution)/shard_map/all_to_all | solution.py:44
  29.3 117.6 %all-gather.5.cloned.1.call-done = bf16[512,3,2304]{2,1,0:T(4,128)(2,1)} async-done(((bf16[1,3,2304]{2,1,0:T(4,128)(2,1)}), bf16[512,3,2304]{2,1,0:T(4,128)(2,1)}) %all-gather.5.cloned.1.call-update) | async-done | bytes 7077904 | tf_op jit(solution)/shard_map/all_gather | solution.py:56
  146.9 17.0 %reshape.170 = bf16[1536,2304]{1,0:T(8,128)(2,1)} reshape(bf16[512,3,2304]{2,1,0:T(4,128)(2,1)} %all-gather.5.cloned.1.call-done) | data formatting | bytes 14155776
  163.9 6.5 %fusion.9 = f32[512,2304]{1,0:T(8,128)S(1)} fusion(bf16[1536,2304]{1,0:T(8,128)(2,1)} %reshape.170, bf16[512,1536]{1,0:T(8,128)(2,1)S(1)} %get-tuple-element.10, f32[1536]{0:T(1024)S(1)} %reduce.2, f32[1536]{0:T(1024)S(1)} %reduce.1, f32[512]{0:T(512)S(1)} %add_rsqrt_fusion.2, f32[512]{0:T(512)S(1)} %broadcast_multiply_fusion), kind=kOutput, calls=%fused_computation.17 | convolution fusion | flops 3628597248 | bytes 13385728 | tf_op jit(solution)/shard_map/dot_general | solution.py:64
  170.4 1.5 slice_multiply_fusion.1
  171.9 1.1 copy-done.2
  174.4 1.9 copy.46
  176.7 1.6 copy.47
  178.4 3.8 %multiply_convert_fusion.1 = (bf16[512,768]{1,0:T(8,128)(2,1)}, bf16[512,768]{1,0:T(8,128)(2,1)S(1)}) fusion(f32[512,768]{1,0:T(8,128)S(1)} %copy.44, f32[512,2304]{1,0:T(8,128)} %copy-done.2, f32[768]{0:T(1024)S(1)} %copy-done.7, f32[768]{0:T(1024)S(1)} %copy-done.8, f32[512,768]{1,0:T(8,128)} %copy.47), kind=kLoop, calls=%fused_computation.27 | loop fusion | flops 2359296 | bytes 7870464 | tf_op jit(solution)/shard_map/convert_element_type | solution.py:65
  182.1 24.8 %all_to_all.20 = bf16[1,32,16,768]{3,2,0,1:T(8,128)(2,1)S(1)} all-to-all(bf16[1,32,16,768]{3,2,0,1:T(8,128)(2,1)S(1)} %bitcast.45), channel_id=1, replica_groups=mesh['grp'=16,'sp'=32] {'sp'}, dimensions={1} | all-to-all | bytes 1572864 | tf_op jit(solution)/shard_map/all_to_all | solution.py:72
  207.0 8.9 %all-to-all-start.2 = ((bf16[1,32,16,768]{3,2,0,1:T(8,128)(2,1)}), bf16[1,32,16,768]{3,2,0,1:T(8,128)(2,1)S(1)}, u32[]{:S(2)}, u32[]{:S(2)}) async-start(bf16[1,32,16,768]{3,2,0,1:T(8,128)(2,1)} %bitcast.8), calls=%async_computation.2 | async-start | bytes 1572864 | tf_op jit(solution)/shard_map/all_to_all | solution.py:69
  216.7 2.4 slice.21
  219.1 16.7 %all-to-all-done.2 = bf16[1,32,16,768]{3,2,0,1:T(8,128)(2,1)S(1)} async-done(((bf16[1,32,16,768]{3,2,0,1:T(8,128)(2,1)}), bf16[1,32,16,768]{3,2,0,1:T(8,128)(2,1)S(1)}, u32[]{:S(2)}, u32[]{:S(2)}) %all-to-all-start.2) | async-done | bytes 786464 | tf_op jit(solution)/shard_map/all_to_all | solution.py:69
  235.8 7.9 %all-to-all-start.1 = ((bf16[1,32,16,768]{3,2,0,1:T(8,128)(2,1)}), bf16[1,32,16,768]{3,2,0,1:T(8,128)(2,1)}, u32[]{:S(2)}, u32[]{:S(2)}) async-start(bf16[1,32,16,768]{3,2,0,1:T(8,128)(2,1)} %bitcast.2), calls=%async_computation.1 | async-start | bytes 1572864 | tf_op jit(solution)/shard_map/all_to_all | solution.py:75
  244.1 1.3 reshape.166
  245.3 3.8 %reshape.164 = bf16[32,16,12,64]{3,2,1,0:T(8,128)(2,1)} reshape(bf16[1,32,16,768]{3,2,0,1:T(8,128)(2,1)} %copy-done.5) | data formatting | bytes 1572864 | tf_op jit(solution)/shard_map/reshape | solution.py:83
  249.1 14.3 %all-to-all-done.1 = bf16[1,32,16,768]{3,2,0,1:T(8,128)(2,1)} async-done(((bf16[1,32,16,768]{3,2,0,1:T(8,128)(2,1)}), bf16[1,32,16,768]{3,2,0,1:T(8,128)(2,1)}, u32[]{:S(2)}, u32[]{:S(2)}) %all-to-all-start.1) | async-done | bytes 786464 | tf_op jit(solution)/shard_map/all_to_all | solution.py:75
  263.4 3.8 %reshape.160 = bf16[32,16,12,64]{3,2,1,0:T(8,128)(2,1)} reshape(bf16[1,32,16,768]{3,2,0,1:T(8,128)(2,1)} %all-to-all-done.1) | data formatting | bytes 1572864 | tf_op jit(solution)/shard_map/reshape | solution.py:85
  267.2 3.7 %fusion.12 = f32[16,12,32,32]{2,3,1,0:T(8,128)S(1)} fusion(bf16[32,16,12,64]{3,2,1,0:T(8,128)(2,1)S(1)} %reshape.166, bf16[32,16,12,64]{3,2,1,0:T(8,128)(2,1)} %reshape.164), kind=kOutput, calls=%fused_computation.20 | convolution fusion | flops 25165824 | bytes 2359296 | tf_op jit(solution)/shard_map/fphd,gphd->phfg/dot_general | solution.py:86
  270.9 1.1 fusion.28
  272.5 1.4 fusion.23
  274.6 2.0 reshape.167
  276.6 7.5 %all-to-all-start.4 = ((bf16[32,1,16,768]{3,2,1,0:T(8,128)(2,1)}), bf16[32,1,16,768]{3,2,1,0:T(8,128)(2,1)S(1)}, u32[]{:S(2)}, u32[]{:S(2)}) async-start(bf16[32,1,16,768]{3,2,1,0:T(8,128)(2,1)} %bitcast.14), calls=%async_computation.4 | async-start | bytes 1572864 | tf_op jit(solution)/shard_map/all_to_all | solution.py:96
  284.1 59.7 %all-gather.7.cloned.1.call-done = bf16[512,3,768]{2,1,0:T(4,128)(2,1)} async-done(((bf16[1,3,768]{2,1,0:T(4,128)(2,1)}), bf16[512,3,768]{2,1,0:T(4,128)(2,1)}) %all-gather.7.cloned.1.call-update) | async-done | bytes 2359312 | tf_op jit(solution)/shard_map/all_gather | solution.py:57
  343.8 6.7 %reshape.172 = bf16[1536,768]{1,0:T(8,128)(2,1)} reshape(bf16[512,3,768]{2,1,0:T(4,128)(2,1)} %all-gather.7.cloned.1.call-done) | data formatting | bytes 4718592
  350.6 4.3 %fusion.7 = bf16[512,1536]{1,0:T(8,128)(2,1)} fusion(bf16[512,768]{1,0:T(8,128)(2,1)S(1)} %bitcast.46, bf16[1536,768]{1,0:T(8,128)(2,1)} %reshape.172, bf16[512,1536]{1,0:T(8,128)(2,1)S(1)} %copy-done.4), kind=kOutput, calls=%fused_computation.13 | convolution fusion | flops 1210318848 | bytes 6291456 | tf_op jit(solution)/shard_map/dot_general | solution.py:100
  (49 shorter events, 7.2 us)
Async XLA Ops:
  6.5 21.5 %copy-start = (bf16[64,1536]{1,0:T(8,128)(2,1)S(1)}, bf16[64,1536]{1,0:T(8,128)(2,1)}, u32[]{:S(2)}) copy-start(bf16[64,1536]{1,0:T(8,128)(2,1)} %param.13) | copy-start | bytes 589828
  6.5 140.3 %all-gather.5.cloned.1.call-start = ((), (), s32[]{:S(2)}) async-start(), calls=%async_computation.5 | async-start | bytes 9455616 | tf_op jit(solution)/shard_map/all_gather | solution.py:56
  9.8 17.6 %all-to-all-start = ((bf16[16,2,256]{2,1,0:T(2,128)(2,1)}), bf16[16,2,256]{2,1,0:T(2,128)(2,1)S(1)}, u32[]{:S(2)}, u32[]{:S(2)}) async-start(bf16[16,2,256]{2,1,0:T(2,128)(2,1)} %reshape.176), calls=%async_computation | async-start | bytes 32768 | tf_op jit(solution)/shard_map/all_to_all | solution.py:44
  28.7 135.2 %copy-start.3 = (bf16[512,1536]{1,0:T(8,128)(2,1)}, bf16[512,1536]{1,0:T(8,128)(2,1)S(1)}, u32[]{:S(2)}) copy-start(bf16[512,1536]{1,0:T(8,128)(2,1)S(1)} %get-tuple-element.10) | copy-start | bytes 4718596
  170.4 2.7 copy-start.2
  176.5 1.8 copy-start.7
  176.5 1.8 copy-start.8
  207.0 36.7 %copy-start.9 = (s32[1,4]{1,0:T(1,128)S(1)}, s32[1,4]{1,0:T(1,128)}, u32[]{:S(2)}) copy-start(s32[1,4]{1,0:T(1,128)} %param.12) | copy-start | bytes 52
  207.0 28.8 %all-to-all-start.2 = ((bf16[1,32,16,768]{3,2,0,1:T(8,128)(2,1)}), bf16[1,32,16,768]{3,2,0,1:T(8,128)(2,1)S(1)}, u32[]{:S(2)}, u32[]{:S(2)}) async-start(bf16[1,32,16,768]{3,2,0,1:T(8,128)(2,1)} %bitcast.8), calls=%async_computation.2 | async-start | bytes 1572864 | tf_op jit(solution)/shard_map/all_to_all | solution.py:69
  215.9 127.9 %all-gather.7.cloned.1.call-start = ((), (), s32[]{:S(2)}) async-start(), calls=%async_computation.6 | async-start | bytes 3151872 | tf_op jit(solution)/shard_map/all_gather | solution.py:57
  235.8 8.2 %copy-start.5 = (bf16[1,32,16,768]{3,2,0,1:T(8,128)(2,1)}, bf16[1,32,16,768]{3,2,0,1:T(8,128)(2,1)S(1)}, u32[]{:S(2)}) copy-start(bf16[1,32,16,768]{3,2,0,1:T(8,128)(2,1)S(1)} %all-to-all-done.2) | copy-start | bytes 2359300
  235.8 27.7 %all-to-all-start.1 = ((bf16[1,32,16,768]{3,2,0,1:T(8,128)(2,1)}), bf16[1,32,16,768]{3,2,0,1:T(8,128)(2,1)}, u32[]{:S(2)}, u32[]{:S(2)}) async-start(bf16[1,32,16,768]{3,2,0,1:T(8,128)(2,1)} %bitcast.2), calls=%async_computation.1 | async-start | bytes 1572864 | tf_op jit(solution)/shard_map/all_to_all | solution.py:75
  270.9 1.6 copy-start.6
  276.6 74.0 %all-to-all-start.4 = ((bf16[32,1,16,768]{3,2,1,0:T(8,128)(2,1)}), bf16[32,1,16,768]{3,2,1,0:T(8,128)(2,1)S(1)}, u32[]{:S(2)}, u32[]{:S(2)}) async-start(bf16[32,1,16,768]{3,2,1,0:T(8,128)(2,1)} %bitcast.14), calls=%async_computation.4 | async-start | bytes 1572864 | tf_op jit(solution)/shard_map/all_to_all | solution.py:96
  284.1 66.5 %copy-start.4 = (bf16[512,1536]{1,0:T(8,128)(2,1)S(1)}, bf16[512,1536]{1,0:T(8,128)(2,1)}, u32[]{:S(2)}) copy-start(bf16[512,1536]{1,0:T(8,128)(2,1)} %copy-done.3) | copy-start | bytes 4718596
  350.6 4.3 %copy-start.1 = (bf16[64,1536]{1,0:T(8,128)(2,1)S(1)}, bf16[64,1536]{1,0:T(8,128)(2,1)}, u32[]{:S(2)}) copy-start(bf16[64,1536]{1,0:T(8,128)(2,1)} %param.13) | copy-start | bytes 589828
Sparse Core Ops, SparseCore 0:
  12.0 134.8 all-gather.4
  221.0 122.8 all-gather.6
where the time goes:
time: 363 us; the launch traced here: 362 us
  waiting for transfers between devices  215 us (59%)
  local copies, waits for them, and re-layouts  46 us (13%)
  starting transfers between devices  34.6 us (10%)
  blocking collectives  24.8 us (7%)
  matrix products  16.5 us (5%)
  between operations  13.6 us (4%)
  other arithmetic  11.5 us (3%)
    all_gather x1, waiting for transfers between devices, local(): lax.all_gather(qkv_weight, ('grp', 'sp'), axis=0, tiled=True)  118 us
    all_gather x1, waiting for transfers between devices, local(): lax.all_gather(out_weight, ('grp', 'sp'), axis=0, tiled=True)  59.7 us
    unnamed x25, local copies, waits for them, and re-layouts  26.5 us
    all_to_all x1, blocking collectives, local(): lax.all_to_all(keys_all.reshape(1, frames, per_block, width), 'sp', split...  24.8 us
    all_to_all x1, waiting for transfers between devices, local(): lax.all_to_all(query.reshape(1, frames, per_block, width), 'sp', split_ax...  16.7 us
    all_to_all x1, waiting for transfers between devices, local(): lax.all_to_all(values_all.reshape(1, frames, per_block, width), 'sp', spl...  14.3 us
    all_to_all x1, starting transfers between devices, local(): lax.all_to_all(coarse_latent, 'grp', split_axis=0, concat_axis=2, tiled=T...  10.2 us
    all_to_all x1, starting transfers between devices, local(): lax.all_to_all(query.reshape(1, frames, per_block, width), 'sp', split_ax...  8.95 us
  transfers between devices with their start and end apart: 6, of which 5 were waited for; matrix products, arithmetic and copies ran while one was open for 9% of the time, Pallas kernels for 0%

commit v1 on v0

v1 whole, which is shorter than its diff:
```python
import jax
import jax.numpy as jnp
from jax import lax
from jax.experimental import pallas as pl
from jax.experimental.pallas import tpu as pltpu
from jax.sharding import PartitionSpec as P

HEADS = 12
HEAD = 64
C = 16
FH = 16
FW = 32
D = 1536
HD = HEADS * HEAD
TOKENS = FH * FW
N_GRP = 16
N_Y = 8
N_SP = 32
BLOCKS = 3 * HD // 128
PAIRS = HEADS // 2
ROWS = 80
PLANE_ROWS = 96

signal_coef = 0.8
noise_coef = 0.6
epsilon = 1e-06
MESH = pl.DeviceIdType.MESH
F32 = jnp.float32
BF16 = jnp.bfloat16


def iota(shape, axis):
    return lax.broadcasted_iota(jnp.int32, shape, axis)


def dot(a, b):
    return jnp.dot(a, b, preferred_element_type=F32)


def dot_t(a, b):
    return lax.dot_general(a, b, (((1,), (1,)), ((), ())), preferred_element_type=F32)


def one_hot(condition):
    return jnp.where(condition, 1.0, 0.0).astype(BF16)


def kernel(
    coarse_ref,
    noise_ref,
    clip_ref,
    embed_ref,
    shift_ref,
    scale_ref,
    w_ref,
    o_ref,
    qg_ref,
    kg_ref,
    out_ref,
    c_recv,
    w_tiles,
    w_cols,
    factors,
    m_own,
    m_all,
    patches,
    z_send,
    z_recv,
    o_tiles,
    o_all,
    perm,
    mixed_rt,
    mixed_tr,
    returned,
    padded_embed,
    hidden,
    c_ss,
    c_rs,
    w_ss,
    w_rs,
    y_ss,
    y_rs,
    d_ss,
    d_rs,
    m_ss,
    m_rs,
    z_ss,
    z_rs,
    p_ss,
    p_rs,
    oy_ss,
    oy_rs,
    od_ss,
    od_rs,
    r_ss,
    r_rs,
):
    g = lax.axis_index("grp")
    s = lax.axis_index("sp")
    y = g // 2
    core = lax.rem(g, 2)
    sibling = g + 1 - 2 * core
    block = (9 * s + 8) // 16
    owner = (16 * block) // 9 == s

    def sp_peer(j):
        return lax.rem(s + j, N_SP)

    def grp_peer(j):
        return lax.rem(g + j, N_GRP)

    def y_peer(j):
        return lax.rem(y + j, N_Y)

    def owner_of(b):
        return (16 * b) // 9

    def remote(src, dst, send_sem, recv_sem, to):
        return pltpu.make_async_remote_copy(
            src_ref=src,
            dst_ref=dst,
            send_sem=send_sem,
            recv_sem=recv_sem,
            device_id=to,
            device_id_type=MESH,
        )

    def loop(start, stop, body):
        def step(j, carry):
            body(j)
            return carry

        lax.fori_loop(start, stop, step, 0)

    def c_copy(to, slot):
        return remote(
            coarse_ref.at[to], c_recv.at[slot], c_ss.at[to], c_rs.at[slot], (to, s)
        )

    def w_copy(b, slot):
        return remote(
            w_ref.at[:, pl.ds(pl.multiple_of(b * 128, 128), 128)],
            w_tiles.at[slot],
            w_ss.at[b],
            w_rs.at[slot],
            (g, owner_of(b)),
        )

    def y_copy(to, slot):
        return remote(
            w_cols.at[y, core], w_cols.at[slot, core], y_ss.at[to], y_rs.at[slot], (2 * to + core, s)
        )

    def d_copy(half):
        return remote(
            w_cols.at[:, half], w_cols.at[:, half], d_ss.at[0], d_rs.at[0], (sibling, s)
        )

    def m_copy(to, b):
        return remote(
            m_own, m_all.at[b, pl.ds(0, ROWS)], m_ss.at[to], m_rs.at[b], (g, to)
        )

    def z_copy(to, slot):
        return remote(
            z_send.at[pl.ds(pl.multiple_of(to * FH, FH), FH)],
            z_recv.at[slot],
            z_ss.at[to],
            z_rs.at[slot],
            (g, to),
        )

    def p_copy(to, slot):
        return remote(o_ref, o_tiles.at[slot], p_ss.at[to], p_rs.at[slot], (g, to))

    def oy_copy(to, slot):
        return remote(
            o_all.at[y, core], o_all.at[slot, core], oy_ss.at[to], oy_rs.at[slot], (2 * to + core, s)
        )

    def od_copy(slot, half):
        return remote(
            o_all.at[slot, half], o_all.at[slot, half], od_ss.at[slot], od_rs.at[slot], (sibling, s)
        )

    def r_copy(to, slot):
        return remote(
            mixed_tr.at[pl.ds(pl.multiple_of(to * FH, FH), FH)],
            returned.at[slot],
            r_ss.at[to],
            r_rs.at[slot],
            (g, to),
        )

    barrier = pltpu.get_barrier_semaphore()

    def greet_sp(j):
        pl.semaphore_signal(barrier, inc=1, device_id=(g, sp_peer(j)), device_id_type=MESH)

    def greet_grp(j):
        pl.semaphore_signal(barrier, inc=1, device_id=(grp_peer(j), s), device_id_type=MESH)

    loop(1, N_SP, greet_sp)
    loop(1, N_GRP, greet_grp)

    embed = embed_ref[...].astype(F32)
    centered = embed - jnp.mean(embed, axis=1, keepdims=True)
    scaled = centered * scale_ref[...]
    scaled_hi = scaled.astype(BF16)
    shift = jnp.where(iota((16, D), 0) == 0, jnp.broadcast_to(shift_ref[...], (16, D)), 0.0)
    shift_hi = shift.astype(BF16)
    factors[pl.ds(0, 64), :] = scaled_hi
    factors[pl.ds(64, 16), :] = shift_hi
    factors[pl.ds(ROWS, 64), :] = (scaled - scaled_hi.astype(F32)).astype(BF16)
    factors[pl.ds(ROWS + 64, 16), :] = (shift - shift_hi.astype(F32)).astype(BF16)
    padded_embed[pl.ds(0, 64), :] = embed_ref[...]
    padded_embed[pl.ds(64, 64), :] = jnp.zeros((64, D), BF16)

    def fill_perm(j):
        base = pl.multiple_of(j * 64, 64)
        row = iota((64, TOKENS), 0) + base
        col = iota((64, TOKENS), 1)
        same = jnp.logical_and(
            jnp.right_shift(row, 5) == jnp.bitwise_and(col, 15),
            jnp.bitwise_and(row, 31) == jnp.right_shift(col, 4),
        )
        perm[pl.ds(base, 64), :] = one_hot(same)

    loop(0, TOKENS // 64, fill_perm)

    def pad_m(j):
        m_all[j, pl.ds(ROWS, 128 - ROWS), :] = jnp.zeros((128 - ROWS, 128), BF16)

    loop(0, BLOCKS, pad_m)

    pl.semaphore_wait(barrier, N_SP - 1 + N_GRP - 1)

    loop(1, N_GRP, lambda j: c_copy(grp_peer(j), g).start())
    c_recv[g] = coarse_ref[g]

    def send_w(j):
        b = lax.rem(j + block, BLOCKS)

        @pl.when(owner_of(b) != s)
        def _():
            w_copy(b, s).start()

    loop(0, BLOCKS, send_w)

    @pl.when(owner)
    def _():
        w_tiles[s] = w_ref[:, pl.ds(pl.multiple_of(block * 128, 128), 128)]

    def wait_c(j):
        c_copy(grp_peer(j), grp_peer(j)).wait_recv()

    loop(1, N_GRP, wait_c)
    lane = iota((FH, 128), 1)
    ones_lane = jnp.where(lane == 64, 1.0, 0.0)
    spread_row = iota((128, 512), 0)
    spread_col = iota((128, 512), 1)
    spread = one_hot(
        jnp.logical_and(
            jnp.right_shift(spread_row, 4) == jnp.right_shift(spread_col, 6),
            jnp.bitwise_and(spread_row, 15) == jnp.bitwise_and(spread_col, 15),
        )
    )
    for k in range(4):
        up = dot(c_recv[:, k, :].astype(BF16), spread)
        noise = noise_ref[:, k * 512 : (k + 1) * 512].astype(F32)
        mix = (signal_coef * up + noise_coef * noise).astype(BF16).astype(F32)
        for half in range(4):
            piece = mix[:, half * 128 : (half + 1) * 128]
            w = k * 8 + half * 2
            patches[w * FH : (w + 1) * FH, :] = jnp.where(lane < 64, piece, 0.0).astype(BF16)
            patches[(w + 1) * FH : (w + 2) * FH, :] = jnp.where(
                lane < 64, pltpu.roll(piece, 64, 1), 0.0
            ).astype(BF16)

    def norm_rows(j):
        rows = pl.ds(pl.multiple_of(j * 64, 64), 64)
        piece = patches[rows, :]
        h = dot(piece, padded_embed[...])
        mean = jnp.mean(h, axis=1, keepdims=True)
        away = h - mean
        var = jnp.mean(away * away, axis=1, keepdims=True)
        z = piece.astype(F32) * lax.rsqrt(var + epsilon)
        z_send[rows, :] = jnp.where(iota((64, 128), 1) == 64, 1.0, z).astype(BF16)

    loop(0, TOKENS // 64, norm_rows)
    loop(1, N_SP, lambda j: z_copy(sp_peer(j), s).start())
    z_recv[s] = z_send[pl.ds(pl.multiple_of(s * FH, FH), FH), :]

    @pl.when(owner)
    def _():
        def wait_w(j):
            w_copy(block, sp_peer(j)).wait_recv()

        loop(1, N_SP, wait_w)
        row = iota((PLANE_ROWS, 512), 0)
        col = iota((PLANE_ROWS, 512), 1)
        within = jnp.bitwise_and(col, 15)
        pick = one_hot(
            jnp.logical_and(within < 3, row == jnp.right_shift(col, 4) * 3 + within)
        )
        w_cols[y, core] = dot(pick, w_tiles[...].reshape(512, 128)).astype(BF16)
        loop(1, N_Y, lambda j: y_copy(y_peer(j), y).start())

    loop(1, N_SP, lambda j: p_copy(sp_peer(j), s).start())
    o_tiles[s] = o_ref[...]

    @pl.when(owner)
    def _():
        loop(1, N_Y, lambda j: y_copy(y_peer(j), y_peer(j)).wait_recv())
        d_copy(core).start()
        d_copy(1 - core).wait_recv()
        both = dot(factors[...], w_cols[...].reshape(D, 128))
        m_own[...] = (both[:ROWS] + both[ROWS:]).astype(BF16)
        loop(1, N_SP, lambda j: m_copy(sp_peer(j), block).start())
        m_all[block, pl.ds(0, ROWS), :] = m_own[...]

    loop(1, N_SP, lambda j: p_copy(sp_peer(j), sp_peer(j)).wait_recv())
    for j in range(HD // 128):
        row = iota((PLANE_ROWS, 1024), 0)
        col = iota((PLANE_ROWS, 1024), 1)
        within = jnp.bitwise_and(col, 31)
        first = jnp.right_shift(col, 5) * 3
        hit = jnp.logical_and(within == j, row == first)
        for i in (1, 2):
            hit = jnp.logical_or(
                hit, jnp.logical_and(within == 6 * i + j, row == first + i)
            )
        o_all[y, core, :, j * 128 : (j + 1) * 128] = dot(
            one_hot(hit), o_tiles[...].reshape(1024, 128)
        ).astype(BF16)
    loop(1, N_Y, lambda j: oy_copy(y_peer(j), y).start())
    od_copy(y, core).start()

    loop(1, N_SP, lambda j: z_copy(sp_peer(j), sp_peer(j)).wait_recv())

    def wait_m(b):
        @pl.when(owner_of(b) != s)
        def _():
            m_copy(owner_of(b), b).wait_recv()

    loop(0, BLOCKS, wait_m)
    z_rt = dot(perm[...], z_recv[...].reshape(TOKENS, 128)).astype(BF16)
    head_row = jnp.bitwise_and(iota((256, 128), 0), 127)
    head_col = iota((256, 128), 1)
    same_head = one_hot(
        jnp.right_shift(head_row, 6) == jnp.right_shift(head_col, 6)
    )
    ones_block = jnp.ones((128, 128), BF16)

    def clip_of(t):
        end = clip_ref[0, 0]
        clip = jnp.where(t >= end, 1, 0)
        for j in (1, 2, 3):
            end = end + clip_ref[0, j]
            clip = clip + jnp.where(t >= end, 1, 0)
        return clip

    mask_row = jnp.bitwise_and(iota((256, 128), 0), 127)
    mask_col = iota((256, 128), 1)
    allowed = jnp.logical_and(
        jnp.right_shift(mask_row, 5) == jnp.right_shift(mask_col, 5),
        clip_of(jnp.bitwise_and(mask_row, 31)) == clip_of(jnp.bitwise_and(mask_col, 31)),
    )
    low_half = iota((128, 128), 1) < 64

    def head_norm(flat, gains):
        squares = flat * flat
        hi = squares.astype(BF16)
        lo = (squares - hi.astype(F32)).astype(BF16)
        total = dot(jnp.concatenate([hi, lo], axis=1), same_head)
        return flat * lax.rsqrt(total * (1.0 / HEAD) + epsilon) * gains

    def pair(j):
        query = head_norm(dot(z_rt, m_all[j]), qg_ref[j]).astype(BF16)
        keys = head_norm(dot(z_rt, m_all[PAIRS + j]), kg_ref[j]).astype(BF16)
        values = dot(z_rt, m_all[2 * PAIRS + j]).astype(BF16)
        for tile in range(4):
            q = query[tile * 128 : (tile + 1) * 128]
            k = keys[tile * 128 : (tile + 1) * 128]
            v = values[tile * 128 : (tile + 1) * 128]
            zero = jnp.zeros_like(q)
            q_two = jnp.concatenate(
                [jnp.where(low_half, q, zero), jnp.where(low_half, zero, q)], axis=0
            )
            scores = jnp.where(allowed, dot_t(q_two, k) * (1.0 / 8.0), -1e30)
            top = jnp.max(scores, axis=1, keepdims=True)
            expo = jnp.exp(scores - top).astype(BF16)
            total = dot(expo, ones_block)
            both = dot(expo, v) / total
            mixed_rt[
                tile * 128 : (tile + 1) * 128, pl.ds(pl.multiple_of(j * 128, 128), 128)
            ] = jnp.where(low_half, both[:128], both[128:]).astype(BF16)

    loop(0, PAIRS, pair)
    for j in range(3):
        cols = slice(j * 256, (j + 1) * 256)
        mixed_tr[:, cols] = lax.dot_general(
            perm[...], mixed_rt[:, cols], (((0,), (0,)), ((), ())), preferred_element_type=F32
        ).astype(BF16)
    loop(1, N_SP, lambda j: r_copy(sp_peer(j), s).start())
    returned[s] = mixed_tr[pl.ds(pl.multiple_of(s * FH, FH), FH), :]

    natural = dot(perm[...], patches[...]).astype(BF16)
    for j in range(6):
        cols = slice(j * 256, (j + 1) * 256)
        hidden[:, cols] = dot(natural, padded_embed[:, cols]).astype(BF16)

    def pass_on(j):
        oy_copy(y_peer(j), y_peer(j)).wait_recv()
        od_copy(y_peer(j), core).start()

    loop(1, N_Y, pass_on)
    loop(1, N_SP, lambda j: r_copy(sp_peer(j), sp_peer(j)).wait_recv())
    loop(0, N_Y, lambda j: od_copy(j, 1 - core).wait_recv())

    for j in range(3):
        cols = slice(j * 256, (j + 1) * 256)
        mixed_rt[:, cols] = dot(perm[...], returned[:, :, cols].reshape(TOKENS, 256)).astype(BF16)
    for j in range(N_Y):
        cols = slice(j * 192, (j + 1) * 192)
        attn = dot_t(mixed_rt[...], o_all[j].reshape(192, HD))
        out_ref[:, cols] = (hidden[:, cols].astype(F32) + attn).astype(BF16)

    loop(1, N_GRP, lambda j: c_copy(grp_peer(j), g).wait_send())

    def end_w(b):
        @pl.when(owner_of(b) != s)
        def _():
            w_copy(b, s).wait_send()

    loop(0, BLOCKS, end_w)

    @pl.when(owner)
    def _():
        loop(1, N_Y, lambda j: y_copy(y_peer(j), y).wait_send())
        d_copy(core).wait_send()
        loop(1, N_SP, lambda j: m_copy(sp_peer(j), block).wait_send())

    loop(1, N_SP, lambda j: z_copy(sp_peer(j), s).wait_send())
    loop(1, N_SP, lambda j: p_copy(sp_peer(j), s).wait_send())
    loop(1, N_Y, lambda j: oy_copy(y_peer(j), y).wait_send())
    loop(0, N_Y, lambda j: od_copy(j, core).wait_send())
    loop(1, N_SP, lambda j: r_copy(sp_peer(j), s).wait_send())


def local(
    coarse_latent,
    renoise,
    clip_frames,
    patch_embed,
    mod_shift,
    mod_scale,
    qkv_weight,
    out_weight,
    q_gain,
    k_gain,
):
    coarse = coarse_latent.reshape(N_GRP, 4, 128).astype(F32)
    coarse = jnp.pad(coarse, ((0, 0), (0, 4), (0, 0)))
    w_rows = jnp.pad(qkv_weight, ((0, 13), (0, 0)))
    o_rows = jnp.pad(out_weight.reshape(18, 128), ((0, 14), (0, 0)))
    vmem = pl.BlockSpec(memory_space=pltpu.VMEM)
    smem = pl.BlockSpec(memory_space=pltpu.SMEM)
    dma = pltpu.SemaphoreType.DMA
    sizes = [16, 16, 32, 32, 8, 8, 1, 1, 32, 32, 32, 32, 32, 32, 8, 8, 8, 8, 32, 32]
    return pl.pallas_call(
        kernel,
        out_shape=jax.ShapeDtypeStruct((TOKENS, D), BF16),
        in_specs=[vmem, vmem, smem] + [vmem] * 7,
        out_specs=vmem,
        scratch_shapes=[
            pltpu.VMEM((N_GRP, 8, 128), F32),
            pltpu.VMEM((N_SP, 16, 128), BF16),
            pltpu.VMEM((N_Y, 2, PLANE_ROWS, 128), BF16),
            pltpu.VMEM((2 * ROWS, D), BF16),
            pltpu.VMEM((ROWS, 128), BF16),
            pltpu.VMEM((BLOCKS, 128, 128), BF16),
            pltpu.VMEM((TOKENS, 128), BF16),
            pltpu.VMEM((TOKENS, 128), BF16),
            pltpu.VMEM((N_SP, FH, 128), BF16),
            pltpu.VMEM((N_SP, 32, 128), BF16),
            pltpu.VMEM((N_Y, 2, PLANE_ROWS, HD), BF16),
            pltpu.VMEM((TOKENS, TOKENS), BF16),
            pltpu.VMEM((TOKENS, HD), BF16),
            pltpu.VMEM((TOKENS, HD), BF16),
            pltpu.VMEM((N_SP, FH, HD), BF16),
            pltpu.VMEM((128, D), BF16),
            pltpu.VMEM((TOKENS, D), BF16),
        ]
        + [dma((n,)) for n in sizes],
        compiler_params=pltpu.CompilerParams(
            collective_id=0, has_side_effects=True, vmem_limit_bytes=48 * 1024 * 1024
        ),
    )(
        coarse,
        renoise,
        clip_frames,
        patch_embed,
        mod_shift,
        mod_scale,
        w_rows,
        o_rows,
        q_gain.reshape(PAIRS, 1, 128),
        k_gain.reshape(PAIRS, 1, 128),
    )


def solution(mesh):
    placed = (
        P(None, "sp", "grp", None),
        P(("grp", "sp"), None),
        P("grp", None),
        P(),
        P("grp", None),
        P("grp", None),
        P(("grp", "sp"), None),
        P(("grp", "sp"), None),
        P(),
        P(),
    )
    return jax.shard_map(
        local, mesh=mesh, in_specs=placed, out_specs=P(("grp", "sp"), None), check_vma=False
    )
```

time: 363 us -> 97 us (0.27)
  waiting for transfers between devices: 215 us -> 0 us
  Pallas kernels: 0 us -> 88 us
  local copies, waits for them, and re-layouts: 46 us -> 8.51 us
  starting transfers between devices: 34.6 us -> 0 us
  blocking collectives: 24.8 us -> 0 us
  matrix products: 16.5 us -> 0 us
  between operations: 13.6 us -> 0.03 us
  other arithmetic: 11.5 us -> 0.01 us
    all_gather x2 -> x0, waiting for transfers between devices: 177 us -> none  [the longest x1 118 us: local(): lax.all_gather(qkv_weight, ('grp', 'sp'), axis=0, tiled=True)]
    pallas_call x0 -> x1, Pallas kernels: none -> 88 us  [local(): pl.pallas_call(kernel, out_shape=jax.ShapeDtypeStruct((TOKENS, D), BF16),...]
    all_to_all x4 -> x0, waiting for transfers between devices: 35.9 us -> none  [the longest x1 16.7 us: local(): lax.all_to_all(query.reshape(1, frames, per_block, width), 'sp', split_ax...]
    all_to_all x4 -> x0, starting transfers between devices: 34.5 us -> none  [the longest x1 10.2 us: local(): lax.all_to_all(coarse_latent, 'grp', split_axis=0, concat_axis=2, tiled=T...]
    all_to_all x1 -> x0, blocking collectives: 24.8 us -> none  [local(): lax.all_to_all(keys_all.reshape(1, frames, per_block, width), 'sp', split...]
    unnamed x25 -> x11, local copies, waits for them, and re-layouts: 26.5 us -> 4.94 us
    dot_general x5 -> x0, matrix products: 16.5 us -> none  [the longest x1 6.53 us: local(): qkv = jnp.dot(normed, qkv_full, preferred_element_type=jnp.float32)]
    reshape x4 -> x3, local copies, waits for them, and re-layouts: 10.8 us -> 2.1 us  [the longest x1 0.71 us: local(): o_rows = jnp.pad(out_weight.reshape(18, 128), ((0, 14), (0, 0)))]
  transfers between devices with their start and end apart: 6 -> 0, of which waited for: 5 -> 0; matrix products, arithmetic and copies ran while one was open for 9% -> 0% of each run, Pallas kernels for 0% -> 0%
where the time goes in v1:
time: 97 us; the launch traced here: 96.5 us
  Pallas kernels  88 us (91%)
  local copies, waits for them, and re-layouts  8.51 us (9%)
    pallas_call x1, Pallas kernels, local(): pl.pallas_call(kernel, out_shape=jax.ShapeDtypeStruct((TOKENS, D), BF16),...  88 us
    unnamed x11, local copies, waits for them, and re-layouts  4.94 us

profile of v1, /device:TPU:1, one launch (start us, length us, event | category | flops | bytes accessed | tf_op | source)
XLA Modules:
  0.0 96.5 jit_solution(7784673018607096595)
XLA Ops:
  0.0 0.7 reshape.13.qg_ref
  0.7 0.7 reshape.14.kg_ref
  1.4 0.7 reshape.12
  2.1 0.7 convert_element_type.10
  2.8 0.7 pad.16.w_ref
  3.6 0.0 copy-start
  3.6 0.9 copy-done
  4.5 0.0 copy-start.1
  4.5 0.8 copy-done.1
  5.4 0.0 copy-start.2
  5.4 0.7 copy-done.2
  6.0 0.0 copy-start.3
  6.0 0.7 copy-done.3
  6.7 0.0 copy-start.4
  6.7 0.7 copy-done.4
  7.4 88.0 %shard_map.100 = bf16[512,1536]{1,0:T(8,128)(2,1)S(1)} custom-call(f32[16,8,128]{2,1,0:T(8,128)S(1)} %pad_convert_fusion.coarse_ref, bf16[16,2048]{1,0:T(8,128)(2,1)S(1)} %copy-done.1, s32[1,4]{1,0:T(1,128)S(1)} %copy-done.4, bf16[64,1536]{1,0:T(8,128)(2,1)S(1)} %copy-done, f32[1,1536]{1,0:T(1,128)S(1)} %copy-done.2, f32[1,1536]{1,0:T(1,128)S(1)} %copy-done.3, ...), custom_call_target="tpu_custom_call" | custom-call | tf_op jit(solution)/shard_map/pallas_call | solution.py:471
  95.4 1.1 %copy.12 = bf16[512,1536]{1,0:T(8,128)(2,1)} copy(bf16[512,1536]{1,0:T(8,128)(2,1)S(1)} %shard_map.100) | data formatting | bytes 3145728
  (2 shorter events, 0.0 us)
Async XLA Ops:
  3.6 0.9 copy-start
  4.5 0.8 copy-start.1
  5.4 0.7 copy-start.2
  6.0 0.7 copy-start.3
  6.7 0.7 copy-start.4

commit v2 on v1

v2 whole, which is shorter than its diff:
```python
import jax
import jax.numpy as jnp
from jax import lax
from jax.experimental import pallas as pl
from jax.experimental.pallas import tpu as pltpu
from jax.sharding import PartitionSpec as P

HEADS = 12
HEAD = 64
C = 16
FH = 16
FW = 32
D = 1536
HD = HEADS * HEAD
TOKENS = FH * FW
WINDOW = 16
N_GRP = 16
N_Y = 8
N_SP = 32
BLOCKS = 3 * HD // 128
PAIRS = HEADS // 2
ROWS = 80
PLANE_ROWS = 96

signal_coef = 0.8
noise_coef = 0.6
epsilon = 1e-06
MESH = pl.DeviceIdType.MESH
F32 = jnp.float32
BF16 = jnp.bfloat16


def iota(shape, axis):
    return lax.broadcasted_iota(jnp.int32, shape, axis)


def dot(a, b):
    return jnp.dot(a, b, preferred_element_type=F32)


def dot_t(a, b):
    return lax.dot_general(a, b, (((1,), (1,)), ((), ())), preferred_element_type=F32)


def one_hot(condition):
    return jnp.where(condition, 1.0, 0.0).astype(BF16)


def kernel(
    coarse_any,
    noise_any,
    clip_any,
    embed_any,
    shift_any,
    scale_any,
    w_any,
    o_any,
    qg_any,
    kg_any,
    out_ref,
    coarse_in,
    noise_ref,
    clip_ref,
    embed_ref,
    shift_ref,
    scale_ref,
    w_in,
    o_in,
    qg_ref,
    kg_ref,
    c_send,
    c_recv,
    w_ref,
    o_wide,
    o_ref,
    w_tiles,
    w_cols,
    factors,
    m_own,
    m_all,
    m_turned,
    patches,
    away_turned,
    z_all,
    z_wide,
    o_tiles,
    o_all,
    perm,
    query,
    dots,
    squares,
    probs,
    blended,
    mixed_turned,
    mixed,
    padded_embed,
    hidden,
    in_s,
    c_ss,
    c_rs,
    w_ss,
    w_rs,
    y_ss,
    y_rs,
    d_ss,
    d_rs,
    m_ss,
    m_rs,
    p_ss,
    p_rs,
    oy_ss,
    oy_rs,
    od_ss,
    od_rs,
    ax_ss,
    ax_rs,
    az_ss,
    az_rs,
    bz_ss,
    bz_rs,
    bx_ss,
    bx_rs,
):
    g = lax.axis_index("grp")
    s = lax.axis_index("sp")
    y = g // 2
    core = lax.rem(g, 2)
    sibling = g + 1 - 2 * core
    x = s // 8
    z = lax.rem(s, 8)
    block = (9 * s + 8) // 16
    owner = (16 * block) // 9 == s

    def sp_peer(j):
        return lax.rem(s + j, N_SP)

    def grp_peer(j):
        return lax.rem(g + j, N_GRP)

    def y_peer(j):
        return lax.rem(y + j, N_Y)

    def x_at(j):
        return lax.rem(x + j + 4, 4)

    def z_at(j):
        return lax.rem(z + j + 8, 8)

    def owner_of(b):
        return (16 * b) // 9

    def remote(src, dst, send_sem, recv_sem, to):
        return pltpu.make_async_remote_copy(
            src_ref=src,
            dst_ref=dst,
            send_sem=send_sem,
            recv_sem=recv_sem,
            device_id=to,
            device_id_type=MESH,
        )

    def loop(start, stop, body):
        def step(j, carry):
            body(j)
            return carry

        lax.fori_loop(start, stop, step, 0)

    def c_copy(to, slot):
        return remote(
            c_send.at[to], c_recv.at[slot], c_ss.at[to], c_rs.at[slot], (to, s)
        )

    def w_copy(b, slot):
        return remote(
            w_ref.at[:, pl.ds(pl.multiple_of(b * 128, 128), 128)],
            w_tiles.at[slot],
            w_ss.at[b],
            w_rs.at[slot],
            (g, owner_of(b)),
        )

    def y_copy(to, slot):
        return remote(
            w_cols.at[y, core], w_cols.at[slot, core], y_ss.at[to], y_rs.at[slot], (2 * to + core, s)
        )

    def d_copy(half):
        return remote(
            w_cols.at[:, half], w_cols.at[:, half], d_ss.at[0], d_rs.at[0], (sibling, s)
        )

    def m_copy(to, b):
        return remote(
            m_own, m_all.at[b, pl.ds(0, ROWS)], m_ss.at[to], m_rs.at[b], (g, to)
        )

    def p_copy(to, slot):
        return remote(o_ref, o_tiles.at[slot], p_ss.at[to], p_rs.at[slot], (g, to))

    def oy_copy(to, slot):
        return remote(
            o_all.at[y, core], o_all.at[slot, core], oy_ss.at[to], oy_rs.at[slot], (2 * to + core, s)
        )

    def od_copy(slot, half):
        return remote(
            o_all.at[slot, half], o_all.at[slot, half], od_ss.at[slot], od_rs.at[slot], (sibling, s)
        )

    def ax_copy(to, slot):
        part = z_all.at[slot, z, pl.ds(0, 32)]
        return remote(part, part, ax_ss.at[to], ax_rs.at[slot], (g, to * 8 + z))

    def az_copy(way, k, first):
        rows = (
            pl.ds(0, 4) if k < 3 else pl.ds(0, 2) if way == 0 else pl.ds(2, 2)
        )
        part = z_all.at[rows, z_at(first), pl.ds(0, 32)]
        to = z_at(1) if way == 0 else z_at(-1)
        return remote(part, part, az_ss.at[way, k], az_rs.at[way, k], (g, x * 8 + to))

    def bz_copy(way, k, first):
        rows = (
            pl.ds(32, 32) if k < 3 else pl.ds(32, 16) if way == 0 else pl.ds(48, 16)
        )
        part = z_all.at[x, z_at(first), rows]
        to = z_at(1) if way == 0 else z_at(-1)
        return remote(part, part, bz_ss.at[way, k], bz_rs.at[way, k], (g, x * 8 + to))

    def bx_copy(way, k, first):
        cols = pl.ds(0, 8) if k == 0 else pl.ds(0, 4) if way == 0 else pl.ds(4, 4)
        part = z_all.at[x_at(first), cols, pl.ds(32, 32)]
        to = x_at(1) if way == 0 else x_at(-1)
        return remote(part, part, bx_ss.at[way, k], bx_rs.at[way, k], (g, to * 8 + z))

    def ring_send(copy, k):
        copy(0, k, -k).start()
        copy(1, k, k).start()

    def ring_wait(copy, k):
        copy(0, k, -1 - k).wait_recv()
        copy(1, k, 1 + k).wait_recv()

    def ring_end(copy, k):
        copy(0, k, -k).wait_send()
        copy(1, k, k).wait_send()

    pairs = [
        (w_any, w_in),
        (coarse_any, coarse_in),
        (o_any, o_in),
        (noise_any, noise_ref),
        (embed_any, embed_ref),
        (scale_any, scale_ref),
        (shift_any, shift_ref),
        (clip_any, clip_ref),
        (qg_any, qg_ref),
        (kg_any, kg_ref),
    ]
    loads = [pltpu.make_async_copy(a, b, in_s.at[i]) for i, (a, b) in enumerate(pairs)]
    for load in loads:
        load.start()

    barrier = pltpu.get_barrier_semaphore()

    def greet_sp(j):
        pl.semaphore_signal(barrier, inc=1, device_id=(g, sp_peer(j)), device_id_type=MESH)

    def greet_grp(j):
        pl.semaphore_signal(barrier, inc=1, device_id=(grp_peer(j), s), device_id_type=MESH)

    loop(1, N_SP, greet_sp)
    loop(1, N_GRP, greet_grp)

    w_ref[...] = jnp.zeros((16, 3 * HD), BF16)
    o_wide[...] = jnp.zeros((32, 128), F32)
    for load in loads[:3]:
        load.wait()
    w_ref[0:3, :] = w_in[...]
    coarse = coarse_in[...].reshape(N_GRP, FW * C).astype(F32)
    for k in range(4):
        c_send[:, k, :] = coarse[:, k * 128 : (k + 1) * 128]
    o_rows = o_in[...].astype(F32)
    for j in range(6):
        o_wide[4 * j : 4 * j + 3, :] = o_rows[:, j * 128 : (j + 1) * 128]
    o_ref[...] = o_wide[...].astype(BF16)

    pl.semaphore_wait(barrier, N_SP - 1 + N_GRP - 1)

    loop(1, N_GRP, lambda j: c_copy(grp_peer(j), g).start())
    c_recv[g] = c_send[g]

    def send_w(j):
        b = lax.rem(j + block, BLOCKS)

        @pl.when(owner_of(b) != s)
        def _():
            w_copy(b, s).start()

    loop(0, BLOCKS, send_w)

    @pl.when(owner)
    def _():
        w_tiles[s] = w_ref[:, pl.ds(pl.multiple_of(block * 128, 128), 128)]

    loop(1, N_SP, lambda j: p_copy(sp_peer(j), s).start())
    o_tiles[s] = o_ref[...]

    for load in loads[3:]:
        load.wait()
    embed = embed_ref[...].astype(F32)
    centered = embed - jnp.mean(embed, axis=1, keepdims=True)
    away_hi = centered.astype(BF16).astype(F32)
    away = jnp.concatenate([away_hi, (centered - away_hi).astype(BF16).astype(F32)], axis=0)
    away_turned[...] = away.T.astype(BF16)
    scaled = centered * scale_ref[...]
    scaled_hi = scaled.astype(BF16)
    shift = jnp.where(iota((16, D), 0) == 0, jnp.broadcast_to(shift_ref[...], (16, D)), 0.0)
    shift_hi = shift.astype(BF16)
    factors[pl.ds(0, 64), :] = scaled_hi
    factors[pl.ds(64, 16), :] = shift_hi
    factors[pl.ds(ROWS, 64), :] = (scaled - scaled_hi.astype(F32)).astype(BF16)
    factors[pl.ds(ROWS + 64, 16), :] = (shift - shift_hi.astype(F32)).astype(BF16)
    padded_embed[pl.ds(0, 64), :] = embed_ref[...]
    padded_embed[pl.ds(64, 64), :] = jnp.zeros((64, D), BF16)
    gains = qg_ref[...] * kg_ref[...] * (1.0 / 8.0)
    gains_turned = jnp.broadcast_to(gains.reshape(1, HD), (128, HD)).T

    def fill_perm(j):
        base = pl.multiple_of(j * 64, 64)
        row = iota((64, TOKENS), 0) + base
        col = iota((64, TOKENS), 1)
        same = jnp.logical_and(
            jnp.right_shift(row, 5) == jnp.bitwise_and(col, 15),
            jnp.bitwise_and(row, 31) == jnp.right_shift(col, 4),
        )
        perm[pl.ds(base, 64), :] = one_hot(same)

    loop(0, TOKENS // 64, fill_perm)

    def pad_m(j):
        m_all[j, pl.ds(ROWS, 128 - ROWS), :] = jnp.zeros((128 - ROWS, 128), BF16)

    loop(0, BLOCKS, pad_m)
    ones_row = one_hot(iota((16, TOKENS), 0) == 0)

    def pad_z(j):
        z_all[j // 8, lax.rem(j, 8), pl.ds(64, 16), :] = ones_row

    loop(0, N_SP, pad_z)

    def pad_blended(j):
        blended[j, pl.ds(64, 16), :] = ones_row

    loop(0, HEADS, pad_blended)

    lane = iota((FH, 128), 1)
    spread_row = iota((128, 512), 0)
    spread_col = iota((128, 512), 1)
    spread = one_hot(
        jnp.logical_and(
            jnp.right_shift(spread_row, 4) == jnp.right_shift(spread_col, 6),
            jnp.bitwise_and(spread_row, 15) == jnp.bitwise_and(spread_col, 15),
        )
    )
    eye = one_hot(iota((128, 128), 0) == iota((128, 128), 1))
    twice = one_hot(jnp.bitwise_and(iota((128, 128), 0), 63) == iota((128, 128), 1))

    def wait_c(j):
        c_copy(grp_peer(j), grp_peer(j)).wait_recv()

    loop(1, N_GRP, wait_c)
    for k in range(4):
        up = dot(c_recv[:, k, :].astype(BF16), spread)
        noise = noise_ref[:, k * 512 : (k + 1) * 512].astype(F32)
        mix = (signal_coef * up + noise_coef * noise).astype(BF16).astype(F32)
        for half in range(4):
            piece = mix[:, half * 128 : (half + 1) * 128]
            w = k * 8 + half * 2
            patches[w * FH : (w + 1) * FH, :] = jnp.where(lane < 64, piece, 0.0).astype(BF16)
            patches[(w + 1) * FH : (w + 2) * FH, :] = jnp.where(
                lane < 64, pltpu.roll(piece, 64, 1), 0.0
            ).astype(BF16)
    turned = dot_t(twice, patches[...])
    turned_two = turned.astype(BF16)
    total = jnp.zeros((1, TOKENS), F32)
    for j in range(6):
        part = dot(away_turned[j * 256 : (j + 1) * 256, :], turned_two)
        total = total + jnp.sum(part * part, axis=0, keepdims=True)
    inverse = lax.rsqrt(total * (1.0 / D) + epsilon)
    z_all[x, z, pl.ds(0, 64), :] = (turned[:64] * inverse).astype(BF16)
    for j in (1, 3, 2):
        ax_copy(x_at(j), x).start()
    ring_send(bz_copy, 0)

    @pl.when(owner)
    def _():
        def wait_w(j):
            w_copy(block, sp_peer(j)).wait_recv()

        loop(1, N_SP, wait_w)
        row = iota((PLANE_ROWS, 512), 0)
        col = iota((PLANE_ROWS, 512), 1)
        within = jnp.bitwise_and(col, 15)
        pick = one_hot(
            jnp.logical_and(within < 3, row == jnp.right_shift(col, 4) * 3 + within)
        )
        w_cols[y, core] = dot(pick, w_tiles[...].reshape(512, 128)).astype(BF16)
        loop(1, N_Y, lambda j: y_copy(y_peer(j), y).start())

    ring_wait(bz_copy, 0)
    ring_send(bz_copy, 1)
    for j in (1, 3, 2):
        ax_copy(x, x_at(j)).wait_recv()
    ring_send(az_copy, 0)

    loop(1, N_SP, lambda j: p_copy(sp_peer(j), sp_peer(j)).wait_recv())
    row = iota((PLANE_ROWS, 1024), 0)
    col = iota((PLANE_ROWS, 1024), 1)
    within = jnp.bitwise_and(col, 31)
    third = jnp.bitwise_and(within, 3)
    fits = jnp.logical_and(third < 3, row == jnp.right_shift(col, 5) * 3 + third)
    for j in range(HD // 128):
        pick = one_hot(jnp.logical_and(fits, jnp.right_shift(within, 2) == j))
        o_all[y, core, :, j * 128 : (j + 1) * 128] = dot(
            pick, o_tiles[...].reshape(1024, 128)
        ).astype(BF16)
    loop(1, N_Y, lambda j: oy_copy(y_peer(j), y).start())
    od_copy(y, core).start()

    ring_wait(bz_copy, 1)
    ring_send(bz_copy, 2)
    ring_wait(az_copy, 0)
    ring_send(az_copy, 1)
    ring_wait(bz_copy, 2)
    ring_send(bz_copy, 3)

    @pl.when(owner)
    def _():
        loop(1, N_Y, lambda j: y_copy(y_peer(j), y_peer(j)).wait_recv())
        d_copy(core).start()
        d_copy(1 - core).wait_recv()
        both = dot(factors[...], w_cols[...].reshape(D, 128))
        m_own[...] = (both[:ROWS] + both[ROWS:]).astype(BF16)
        loop(1, N_SP, lambda j: m_copy(sp_peer(j), block).start())
        m_all[block, pl.ds(0, ROWS), :] = m_own[...]

    ring_wait(bz_copy, 3)
    ring_send(bx_copy, 0)
    ring_wait(az_copy, 1)
    ring_send(az_copy, 2)

    natural = dot(perm[...], patches[...]).astype(BF16)
    for j in range(6):
        cols = slice(j * 256, (j + 1) * 256)
        hidden[:, cols] = dot(natural, padded_embed[:, cols]).astype(BF16)

    ring_wait(az_copy, 2)
    ring_send(az_copy, 3)
    ring_wait(bx_copy, 0)
    bx_copy(0, 1, -1).start()
    bx_copy(1, 1, 1).start()

    def wait_m(b):
        @pl.when(owner_of(b) != s)
        def _():
            m_copy(owner_of(b), b).wait_recv()

        m_turned[pl.ds(pl.multiple_of(b * 128, 128), 128), :] = dot_t(eye, m_all[b])[
            :, :ROWS
        ].astype(BF16)

    loop(0, BLOCKS, wait_m)
    own = z_all[x, z]
    for j in range(PAIRS):
        rows = slice(j * 128, (j + 1) * 128)
        q = dot(m_turned[rows, :], own).reshape(2, HEAD, TOKENS)
        level = jnp.sum(q * q, axis=1, keepdims=True) * (1.0 / HEAD) + epsilon
        q = (q * lax.rsqrt(level)).reshape(128, TOKENS)
        gain = jnp.concatenate([gains_turned[rows]] * 4, axis=1)
        query[rows, :] = q * gain

    def pass_on(j):
        oy_copy(y_peer(j), y_peer(j)).wait_recv()
        od_copy(y_peer(j), core).start()

    loop(1, N_Y, pass_on)

    ring_wait(az_copy, 3)
    bx_copy(0, 1, -2).wait_recv()
    bx_copy(1, 1, 2).wait_recv()

    ends = [clip_ref[0, 0]]
    for j in (1, 2, 3):
        ends.append(ends[-1] + clip_ref[0, j])
    first = jnp.int32(0)
    last = ends[0]
    for j in (1, 2, 3):
        inside = s >= ends[j - 1]
        first = jnp.where(inside, ends[j - 1], first)
        last = jnp.where(inside, ends[j], last)
    base = jnp.minimum(first, N_SP - WINDOW)

    def frame(j):
        t = base + j
        entries = z_all[jnp.right_shift(t, 3), jnp.bitwise_and(t, 7)]
        z_wide[j] = entries[:64].astype(F32)
        for pair in range(PAIRS):
            rows = slice(pair * 128, (pair + 1) * 128)
            k = dot(m_turned[HD + pair * 128 : HD + (pair + 1) * 128, :], entries)
            dots[j, pl.ds(2 * pair, 2), :] = jnp.sum(
                (k * query[rows, :]).reshape(2, HEAD, TOKENS), axis=1
            )
            squares[j, pl.ds(2 * pair, 2), :] = jnp.sum(
                (k * k).reshape(2, HEAD, TOKENS), axis=1
            )

    loop(0, WINDOW, frame)
    order = iota((WINDOW, HEADS, TOKENS), 0) + base
    valid = jnp.logical_and(order >= first, order < last)
    scores = dots[...] * lax.rsqrt(squares[...] * (1.0 / HEAD) + epsilon)
    scores = jnp.where(valid, scores, -1e30)
    expo = jnp.exp(scores - jnp.max(scores, axis=0, keepdims=True))
    probs[...] = expo / jnp.sum(expo, axis=0, keepdims=True)

    def head(h):
        total = jnp.zeros((HEAD, TOKENS), F32)
        for j in range(WINDOW):
            total = total + probs[j, pl.ds(h, 1), :] * z_wide[j]
        blended[h, pl.ds(0, 64), :] = total.astype(BF16)
        rows = pl.ds(pl.multiple_of(h * HEAD, HEAD), HEAD)
        value_rows = pl.ds(pl.multiple_of(2 * HD + h * HEAD, HEAD), HEAD)
        mixed_turned[rows, :] = dot(m_turned[value_rows, :], blended[h]).astype(BF16)

    loop(0, HEADS, head)

    loop(0, N_Y, lambda j: od_copy(j, 1 - core).wait_recv())
    for j in range(3):
        cols = slice(j * 256, (j + 1) * 256)
        mixed[:, cols] = dot_t(perm[...], mixed_turned[cols, :]).astype(BF16)
    for j in range(N_Y):
        cols = slice(j * 192, (j + 1) * 192)
        attn = dot_t(mixed[...], o_all[j].reshape(192, HD))
        out_ref[:, cols] = (hidden[:, cols].astype(F32) + attn).astype(BF16)

    loop(1, N_GRP, lambda j: c_copy(grp_peer(j), g).wait_send())

    def end_w(b):
        @pl.when(owner_of(b) != s)
        def _():
            w_copy(b, s).wait_send()

    loop(0, BLOCKS, end_w)

    @pl.when(owner)
    def _():
        loop(1, N_Y, lambda j: y_copy(y_peer(j), y).wait_send())
        d_copy(core).wait_send()
        loop(1, N_SP, lambda j: m_copy(sp_peer(j), block).wait_send())

    loop(1, N_SP, lambda j: p_copy(sp_peer(j), s).wait_send())
    loop(1, N_Y, lambda j: oy_copy(y_peer(j), y).wait_send())
    loop(0, N_Y, lambda j: od_copy(j, core).wait_send())
    for j in (1, 3, 2):
        ax_copy(x_at(j), x).wait_send()
    for k in range(4):
        ring_end(az_copy, k)
        ring_end(bz_copy, k)
    ring_end(bx_copy, 0)
    bx_copy(0, 1, -1).wait_send()
    bx_copy(1, 1, 1).wait_send()


def local(
    coarse_latent,
    renoise,
    clip_frames,
    patch_embed,
    mod_shift,
    mod_scale,
    qkv_weight,
    out_weight,
    q_gain,
    k_gain,
):
    dma = pltpu.SemaphoreType.DMA
    sems = [10, 16, 16, 32, 32, 8, 8, 1, 1, 32, 32, 32, 32, 8, 8, 8, 8, 4, 4]
    rings = [(2, 4)] * 4 + [(2, 2)] * 2
    args = (
        coarse_latent,
        renoise,
        clip_frames,
        patch_embed,
        mod_shift,
        mod_scale,
        qkv_weight,
        out_weight,
        q_gain,
        k_gain,
    )
    inputs = [
        (pltpu.SMEM if a.dtype == jnp.int32 else pltpu.VMEM)(a.shape, a.dtype) for a in args
    ]
    return pl.pallas_call(
        kernel,
        out_shape=jax.ShapeDtypeStruct((TOKENS, D), BF16),
        in_specs=[pl.BlockSpec(memory_space=pl.ANY)] * len(args),
        out_specs=pl.BlockSpec(memory_space=pltpu.VMEM),
        scratch_shapes=inputs
        + [
            pltpu.VMEM((N_GRP, 8, 128), F32),
            pltpu.VMEM((N_GRP, 8, 128), F32),
            pltpu.VMEM((16, 3 * HD), BF16),
            pltpu.VMEM((32, 128), F32),
            pltpu.VMEM((32, 128), BF16),
            pltpu.VMEM((N_SP, 16, 128), BF16),
            pltpu.VMEM((N_Y, 2, PLANE_ROWS, 128), BF16),
            pltpu.VMEM((2 * ROWS, D), BF16),
            pltpu.VMEM((ROWS, 128), BF16),
            pltpu.VMEM((BLOCKS, 128, 128), BF16),
            pltpu.VMEM((3 * HD, ROWS), BF16),
            pltpu.VMEM((TOKENS, 128), BF16),
            pltpu.VMEM((D, 128), BF16),
            pltpu.VMEM((4, 8, ROWS, TOKENS), BF16),
            pltpu.VMEM((WINDOW, HEAD, TOKENS), F32),
            pltpu.VMEM((N_SP, 32, 128), BF16),
            pltpu.VMEM((N_Y, 2, PLANE_ROWS, HD), BF16),
            pltpu.VMEM((TOKENS, TOKENS), BF16),
            pltpu.VMEM((HD, TOKENS), F32),
            pltpu.VMEM((WINDOW, HEADS, TOKENS), F32),
            pltpu.VMEM((WINDOW, HEADS, TOKENS), F32),
            pltpu.VMEM((WINDOW, HEADS, TOKENS), F32),
            pltpu.VMEM((HEADS, ROWS, TOKENS), BF16),
            pltpu.VMEM((HD, TOKENS), BF16),
            pltpu.VMEM((TOKENS, HD), BF16),
            pltpu.VMEM((128, D), BF16),
            pltpu.VMEM((TOKENS, D), BF16),
        ]
        + [dma((n,)) for n in sems]
        + [dma(n) for n in rings],
        compiler_params=pltpu.CompilerParams(
            collective_id=0, has_side_effects=True, vmem_limit_bytes=48 * 1024 * 1024
        ),
    )(*args)


def solution(mesh):
    placed = (
        P(None, "sp", "grp", None),
        P(("grp", "sp"), None),
        P("grp", None),
        P(),
        P("grp", None),
        P("grp", None),
        P(("grp", "sp"), None),
        P(("grp", "sp"), None),
        P(),
        P(),
    )
    return jax.shard_map(
        local, mesh=mesh, in_specs=placed, out_specs=P(("grp", "sp"), None), check_vma=False
    )
```

time: 97 us -> 82.9 us (0.85)
  Pallas kernels: 88 us -> 74 us
    pallas_call x1, Pallas kernels: 88 us -> 74 us  [local(): pl.pallas_call(kernel, out_shape=jax.ShapeDtypeStruct((TOKENS, D), BF16),...]
    unnamed x11 -> x20, local copies, waits for them, and re-layouts: 4.94 us -> 8.47 us
    reshape x3 -> x0, local copies, waits for them, and re-layouts: 2.1 us -> none  [the longest x1 0.71 us: local(): o_rows = jnp.pad(out_weight.reshape(18, 128), ((0, 14), (0, 0)))]
where the time goes in v2:
time: 82.9 us; the launch traced here: 82.5 us
  Pallas kernels  74 us (89%)
  local copies, waits for them, and re-layouts  8.47 us (10%)
    pallas_call x1, Pallas kernels, local(): pl.pallas_call(kernel, out_shape=jax.ShapeDtypeStruct((TOKENS, D), BF16),...  74 us
    unnamed x20, local copies, waits for them, and re-layouts  8.47 us

profile of v2, /device:TPU:1, one launch (start us, length us, event | category | flops | bytes accessed | tf_op | source)
XLA Modules:
  0.0 82.5 jit_solution(855956676313877400)
XLA Ops:
  0.0 0.7 copy.11.coarse_any
  0.7 0.0 copy-start
  0.8 0.9 %copy-done = bf16[64,1536]{1,0:T(8,128)(2,1)S(1)} copy-done((bf16[64,1536]{1,0:T(8,128)(2,1)S(1)}, bf16[64,1536]{1,0:T(8,128)(2,1)}, u32[]{:S(2)}) %copy-start) | copy-done | bytes 196632
  1.7 0.0 copy-start.1
  1.7 0.8 %copy-done.1 = bf16[16,2048]{1,0:T(8,128)(2,1)S(1)} copy-done((bf16[16,2048]{1,0:T(8,128)(2,1)S(1)}, bf16[16,2048]{1,0:T(8,128)(2,1)}, u32[]{:S(2)}) %copy-start.1) | copy-done | bytes 65560
  2.5 0.0 copy-start.2
  2.5 0.7 copy-done.2
  3.2 0.0 copy-start.3
  3.2 0.7 copy-done.3
  3.9 0.0 copy-start.4
  3.9 0.7 copy-done.4
  4.6 0.0 copy-start.5
  4.6 0.7 copy-done.5
  5.3 0.0 copy-start.6
  5.3 0.7 copy-done.6
  6.0 0.0 copy-start.7
  6.0 0.7 copy-done.7
  6.7 0.0 copy-start.8
  6.7 0.7 copy-done.8
  7.3 74.0 %shard_map.100 = bf16[512,1536]{1,0:T(8,128)(2,1)S(1)} custom-call(bf16[16,1,1,512]{3,2,1,0:T(2,128)(2,1)S(1)} %copy.11.coarse_any, bf16[16,2048]{1,0:T(8,128)(2,1)S(1)} %copy-done.1, s32[1,4]{1,0:T(1,128)S(1)} %copy-done.8, bf16[64,1536]{1,0:T(8,128)(2,1)S(1)} %copy-done, f32[1,1536]{1,0:T(1,128)S(1)} %copy-done.3, f32[1,1536]{1,0:T(1,128)S(1)} %copy-done.4, ...), custom_call_target="tpu_custom_call" | custom-call | tf_op jit(solution)/shard_map/pallas_call | solution.py:605
  81.3 1.1 %copy.13 = bf16[512,1536]{1,0:T(8,128)(2,1)} copy(bf16[512,1536]{1,0:T(8,128)(2,1)S(1)} %shard_map.100) | data formatting | bytes 3145728
Async XLA Ops:
  0.7 0.9 %copy-start = (bf16[64,1536]{1,0:T(8,128)(2,1)S(1)}, bf16[64,1536]{1,0:T(8,128)(2,1)}, u32[]{:S(2)}) copy-start(bf16[64,1536]{1,0:T(8,128)(2,1)} %embed_any.1) | copy-start | bytes 589828
  1.7 0.8 %copy-start.1 = (bf16[16,2048]{1,0:T(8,128)(2,1)S(1)}, bf16[16,2048]{1,0:T(8,128)(2,1)}, u32[]{:S(2)}) copy-start(bf16[16,2048]{1,0:T(8,128)(2,1)} %noise_any.1) | copy-start | bytes 196612
  2.5 0.7 copy-start.2
  3.2 0.7 copy-start.3
  3.9 0.7 copy-start.4
  4.6 0.7 copy-start.5
  5.3 0.7 copy-start.6
  6.0 0.7 copy-start.7
  6.7 0.7 copy-start.8

commit v3 on v2

v3 whole, which is shorter than its diff:
```python
import jax
import jax.numpy as jnp
from jax import lax
from jax.experimental import pallas as pl
from jax.experimental.pallas import tpu as pltpu
from jax.sharding import PartitionSpec as P

HEADS = 12
HEAD = 64
C = 16
FH = 16
FW = 32
D = 1536
HD = HEADS * HEAD
TOKENS = FH * FW
WINDOW = 16
N_GRP = 16
N_Y = 8
N_SP = 32
BLOCKS = 3 * HD // 128
PAIRS = HEADS // 2
ROWS = 80
PLANE_ROWS = 96

signal_coef = 0.8
noise_coef = 0.6
epsilon = 1e-06
MESH = pl.DeviceIdType.MESH
F32 = jnp.float32
BF16 = jnp.bfloat16


def iota(shape, axis):
    return lax.broadcasted_iota(jnp.int32, shape, axis)


def dot(a, b):
    return jnp.dot(a, b, preferred_element_type=F32)


def dot_t(a, b):
    return lax.dot_general(a, b, (((1,), (1,)), ((), ())), preferred_element_type=F32)


def one_hot(condition):
    return jnp.where(condition, 1.0, 0.0).astype(BF16)


def kernel(
    coarse_any,
    noise_any,
    clip_any,
    embed_any,
    shift_any,
    scale_any,
    w_any,
    o_any,
    qg_any,
    kg_any,
    out_ref,
    coarse_in,
    noise_ref,
    clip_ref,
    embed_ref,
    shift_ref,
    scale_ref,
    w_in,
    o_in,
    qg_ref,
    kg_ref,
    c_send,
    c_recv,
    w_ref,
    o_wide,
    o_ref,
    w_tiles,
    w_cols,
    sibling_scale,
    sibling_shift,
    factors,
    m_own,
    m_all,
    m_turned,
    patches,
    noise_rows,
    coarse_rows,
    cov,
    n_near,
    n_far,
    k_near,
    k_far,
    z_wide,
    o_tiles,
    o_own,
    o_bands,
    o_all,
    perm,
    query,
    keys_a,
    keys_b,
    dots,
    squares,
    probs,
    blended,
    mixed_turned,
    mixed,
    padded_embed,
    hidden,
    in_s,
    c_ss,
    c_rs,
    w_ss,
    w_rs,
    y_ss,
    y_rs,
    d_ss,
    d_rs,
    m_ss,
    m_rs,
    pz_ss,
    pz_rs,
    px_ss,
    px_rs,
    od_ss,
    od_rs,
    kz_ss,
    kz_rs,
    kx_ss,
    kx_rs,
    o2_ss,
    o2_rs,
    n2_ss,
    n2_rs,
    nr_ss,
    nr_rs,
    nx_ss,
    nx_rs,
):
    g = lax.axis_index("grp")
    s = lax.axis_index("sp")
    y = g // 2
    core = lax.rem(g, 2)
    sibling = g + 1 - 2 * core
    x = s // 8
    z = lax.rem(s, 8)
    half = z // 4
    place = x * 4 + lax.rem(z, 4)
    first_pick = lax.rem(place, 2) == core
    owner = jnp.logical_or(first_pick, jnp.logical_or(place == 12, place == 13))
    block = jnp.where(first_pick, place, place + 4)
    plane = core * N_SP + s

    def sp_peer(j):
        return lax.rem(s + j, N_SP)

    def grp_peer(j):
        return lax.rem(g + j, N_GRP)

    def y_peer(j):
        return lax.rem(y + j, N_Y)

    def x_at(j):
        return lax.rem(x + j + 4, 4)

    def z_at(j):
        return lax.rem(z + j + 8, 8)

    def owner_core(b):
        return jnp.where(b < 16, lax.rem(b, 2), 1 - lax.rem(b, 2))

    def owner_sp(b, part):
        q = jnp.where(b < 16, b, b - 4)
        return (q // 4) * 8 + part * 4 + lax.rem(q, 4)

    def not_here(b, part):
        return jnp.logical_or(owner_core(b) != core, owner_sp(b, part) != s)

    def remote(src, dst, send_sem, recv_sem, to):
        return pltpu.make_async_remote_copy(
            src_ref=src,
            dst_ref=dst,
            send_sem=send_sem,
            recv_sem=recv_sem,
            device_id=to,
            device_id_type=MESH,
        )

    def loop(start, stop, body):
        def step(j, carry):
            body(j)
            return carry

        lax.fori_loop(start, stop, step, 0)

    def c_copy(to, slot):
        return remote(
            c_send.at[to], c_recv.at[slot], c_ss.at[to], c_rs.at[slot], (to, s)
        )

    def w_copy(b, part, slot):
        return remote(
            w_ref.at[:, pl.ds(pl.multiple_of(b * 128, 128), 128)],
            w_tiles.at[slot],
            w_ss.at[2 * b + part],
            w_rs.at[slot],
            (2 * y + owner_core(b), owner_sp(b, part)),
        )

    def y_copy(to, slot):
        return remote(
            w_cols.at[y], w_cols.at[slot], y_ss.at[to], y_rs.at[slot], (2 * to + core, s)
        )

    def d_copies():
        to = (sibling, s)
        return [
            remote(scale_ref, sibling_scale, d_ss.at[0], d_rs.at[0], to),
            remote(shift_ref, sibling_shift, d_ss.at[1], d_rs.at[1], to),
        ]

    def m_target(i):
        return i // 16, (lax.rem(i, 16) // 4) * 8 + half * 4 + lax.rem(i, 4)

    def m_copy(i, b):
        at_core, at_sp = m_target(i)
        return remote(
            m_own.at[at_core],
            m_all.at[b, pl.ds(0, ROWS)],
            m_ss.at[i],
            m_rs.at[b],
            (2 * y + at_core, at_sp),
        )

    def pz_copy(to, slot):
        return remote(o_ref, o_tiles.at[slot], pz_ss.at[to], pz_rs.at[slot], (g, x * 8 + to))

    def px_copy(to, slot):
        return remote(o_own, o_bands.at[slot], px_ss.at[to], px_rs.at[slot], (g, to * 8 + z))

    def od_copy(slot, half):
        return remote(
            o_all.at[slot, half], o_all.at[slot, half], od_ss.at[slot], od_rs.at[slot], (sibling, s)
        )

    def kz_copy(to, slot):
        part = k_near.at[1, slot]
        return remote(part, part, kz_ss.at[to], kz_rs.at[slot], (g, x * 8 + to))

    def kx_copy(way, k):
        if k == 0:
            src, dst = k_near.at[1], k_near.at[2 * way]
        else:
            half_row = pl.ds(4 * way, 4)
            src, dst = k_near.at[2 * way, half_row], k_far.at[half_row]
        to = x_at(1) if way == 0 else x_at(-1)
        return remote(src, dst, kx_ss.at[way, k], kx_rs.at[way, k], (g, to * 8 + z))

    moves = [(1, 0, 0), (-1, 0, 0), (2, 0, 0), (-2, 0, 0), (1, -2, 0), (-1, 2, 0), (2, -2, 1), (-2, 2, 2)]

    def ring_copy(view, at, to, sems, i, start):
        part = view(at(start), moves[i][2])
        return remote(part, part, sems[0].at[i], sems[1].at[i], to(at(moves[i][0])))

    def ring_send(ring, i):
        ring_copy(*ring, i, moves[i][1]).start()

    def ring_wait(ring, i):
        ring_copy(*ring, i, moves[i][1] - moves[i][0]).wait_recv()

    def ring_end(ring, i):
        ring_copy(*ring, i, moves[i][1]).wait_send()

    def o_view(slot, part):
        rows = (pl.ds(0, PLANE_ROWS), pl.ds(0, 48), pl.ds(48, 48))[part]
        return o_all.at[slot, core, rows]

    def n_view(slot, part):
        rows = (pl.ds(0, 64), pl.ds(0, 32), pl.ds(32, 32))[part]
        return n_near.at[1, slot, rows]

    def y_at(j):
        return lax.rem(y + j + N_Y, N_Y)

    o_ring = (o_view, y_at, lambda to: (2 * to + core, s), (o2_ss, o2_rs))
    n_ring = (n_view, z_at, lambda to: (g, x * 8 + to), (n2_ss, n2_rs))

    offsets = [0, -1, 1, -2, 2, -3, 3, -4]

    def nx_copy(way, i):
        slot = z_at(offsets[i])
        to = x_at(1) if way == 0 else x_at(-1)
        return remote(
            n_near.at[1, slot],
            n_near.at[2 * way, slot],
            nx_ss.at[way, i],
            nx_rs.at[way, i],
            (g, to * 8 + z),
        )

    def nr_copy(i):
        slot = z_at(offsets[i])
        way = i % 2
        to = x_at(1) if way == 0 else x_at(-1)
        return remote(
            n_near.at[2 * way, slot], n_far.at[slot], nr_ss.at[i], nr_rs.at[i], (g, to * 8 + z)
        )

    def spread_frames(indices):
        for i in indices:
            nx_copy(0, i).start()
            nx_copy(1, i).start()

    def relay_frames(indices):
        for i in indices:
            nx_copy(0, i).wait_recv()
            nx_copy(1, i).wait_recv()
            nr_copy(i).start()

    pairs = [
        (w_any, w_in),
        (coarse_any, coarse_in),
        (o_any, o_in),
        (noise_any, noise_ref),
        (scale_any, scale_ref),
        (shift_any, shift_ref),
        (embed_any, embed_ref),
        (clip_any, clip_ref),
        (qg_any, qg_ref),
        (kg_any, kg_ref),
    ]
    loads = [pltpu.make_async_copy(a, b, in_s.at[i]) for i, (a, b) in enumerate(pairs)]
    for load in loads:
        load.start()

    barrier = pltpu.get_barrier_semaphore()

    def greet_plane(j):
        other = lax.rem(plane + j, 2 * N_SP)
        pl.semaphore_signal(
            barrier,
            inc=1,
            device_id=(2 * y + other // N_SP, lax.rem(other, N_SP)),
            device_id_type=MESH,
        )

    def greet_y(j):
        for c in (0, 1):
            pl.semaphore_signal(
                barrier, inc=1, device_id=(2 * y_peer(j) + c, s), device_id_type=MESH
            )

    loop(1, 2 * N_SP, greet_plane)
    loop(1, N_Y, greet_y)

    w_ref[...] = jnp.zeros((16, 3 * HD), BF16)
    o_wide[...] = jnp.zeros((32, 128), F32)
    for load in loads[:6]:
        load.wait()
    w_ref[0:3, :] = w_in[...]
    coarse = coarse_in[...].astype(F32)
    for k in range(4):
        c_send[:, k, :] = coarse[:, k * 128 : (k + 1) * 128]
    o_rows = o_in[...].astype(F32)
    for j in range(6):
        o_wide[4 * j : 4 * j + 3, :] = o_rows[:, j * 128 : (j + 1) * 128]
    o_ref[...] = o_wide[...].astype(BF16)

    lane = iota((FH, 128), 1)
    eye = one_hot(iota((128, 128), 0) == iota((128, 128), 1))

    def to_positions(ref, k, piece):
        ref[2 * k * FH : (2 * k + 1) * FH, :] = jnp.where(lane < 64, piece, 0.0).astype(BF16)
        ref[(2 * k + 1) * FH : (2 * k + 2) * FH, :] = jnp.where(
            lane < 64, pltpu.roll(piece, 64, 1), 0.0
        ).astype(BF16)

    for k in range(16):
        to_positions(noise_rows, k, noise_ref[:, k * 128 : (k + 1) * 128].astype(F32))
    n_near[1, z] = dot_t(eye[:64], noise_rows[...]).astype(BF16)

    pl.semaphore_wait(barrier, 2 * N_SP - 1 + 2 * (N_Y - 1))

    loop(1, N_GRP, lambda j: c_copy(grp_peer(j), g).start())
    c_recv[g] = c_send[g]
    for copy in d_copies():
        copy.start()

    def send_w(j):
        m = lax.rem(j + 4 * place, 2 * BLOCKS)
        b = m // 2
        part = lax.rem(m, 2)

        @pl.when(not_here(b, part))
        def _():
            w_copy(b, part, plane).start()

    loop(0, 2 * BLOCKS, send_w)

    @pl.when(owner)
    def _():
        w_tiles[plane] = w_ref[:, pl.ds(pl.multiple_of(block * 128, 128), 128)]

    for j in (4, 3, 5, 2, 6, 1, 7):
        pz_copy(z_at(j), z).start()
    o_tiles[z] = o_ref[...]

    for load in loads[6:]:
        load.wait()
    embed = embed_ref[...].astype(F32)
    centered = embed - jnp.mean(embed, axis=1, keepdims=True)
    away_hi = centered.astype(BF16)
    away = jnp.concatenate([away_hi, (centered - away_hi.astype(F32)).astype(BF16)], axis=0)
    gram = dot_t(away, away) * (1.0 / D)
    gram = gram[:64] + gram[64:]
    gram = (gram + pltpu.roll(gram, 64, 1))[:, :64]
    for j in range(3):
        part = gram.astype(BF16)
        cov[j * 64 : (j + 1) * 64, :] = part
        gram = gram - part.astype(F32)

    def set_factors(at, scale, shift):
        scaled = centered * scale
        scaled_hi = scaled.astype(BF16)
        shift = jnp.where(iota((16, D), 0) == 0, jnp.broadcast_to(shift, (16, D)), 0.0)
        shift_hi = shift.astype(BF16)
        factors[at, pl.ds(0, 64), :] = scaled_hi
        factors[at, pl.ds(64, 16), :] = shift_hi
        factors[at, pl.ds(ROWS, 64), :] = (scaled - scaled_hi.astype(F32)).astype(BF16)
        factors[at, pl.ds(ROWS + 64, 16), :] = (shift - shift_hi.astype(F32)).astype(BF16)

    for copy in d_copies():
        copy.wait_recv()

    @pl.when(owner)
    def _():
        set_factors(core, scale_ref[...], shift_ref[...])
        set_factors(1 - core, sibling_scale[...], sibling_shift[...])

    padded_embed[pl.ds(0, 64), :] = embed_ref[...]
    padded_embed[pl.ds(64, 64), :] = jnp.zeros((64, D), BF16)
    gains = qg_ref[...] * kg_ref[...] * (1.0 / 8.0)
    gains_turned = jnp.broadcast_to(gains.reshape(1, HD), (128, HD)).T

    def fill_perm(j):
        base = pl.multiple_of(j * 64, 64)
        row = iota((64, TOKENS), 0) + base
        col = iota((64, TOKENS), 1)
        same = jnp.logical_and(
            jnp.right_shift(row, 5) == jnp.bitwise_and(col, 15),
            jnp.bitwise_and(row, 31) == jnp.right_shift(col, 4),
        )
        perm[pl.ds(base, 64), :] = one_hot(same)

    loop(0, TOKENS // 64, fill_perm)

    def pad_m(j):
        m_all[j, pl.ds(ROWS, 128 - ROWS), :] = jnp.zeros((128 - ROWS, 128), BF16)

    loop(0, BLOCKS, pad_m)
    ones_row = one_hot(iota((16, TOKENS), 0) == 0)

    def pad_blended(j):
        blended[j, pl.ds(64, 16), :] = ones_row

    loop(0, HEADS, pad_blended)

    for i in range(4):
        ring_send(n_ring, i)
    spread_frames([0])

    @pl.when(owner)
    def _():
        def wait_w(j):
            w_copy(block, half, lax.rem(plane + j, 2 * N_SP)).wait_recv()

        loop(1, 2 * N_SP, wait_w)
        row = iota((2 * PLANE_ROWS, 1024), 0)
        col = iota((2 * PLANE_ROWS, 1024), 1)
        within = jnp.bitwise_and(col, 15)
        pick = one_hot(
            jnp.logical_and(within < 3, row == jnp.right_shift(col, 4) * 3 + within)
        )
        w_cols[y] = dot(pick, w_tiles[...].reshape(1024, 128)).astype(BF16)
        loop(1, N_Y, lambda j: y_copy(y_peer(j), y).start())

    for j in (1, 7, 2, 6, 3, 5, 4):
        pz_copy(z, z_at(j)).wait_recv()
    row = iota((144, 256), 0)
    col = iota((144, 256), 1)
    third = jnp.bitwise_and(col, 3)
    column = jnp.right_shift(jnp.bitwise_and(col, 31), 2)
    pick_rows = one_hot(
        jnp.logical_and(third < 3, row == column * 24 + jnp.right_shift(col, 5) * 3 + third)
    )
    o_own[...] = dot(pick_rows, o_tiles[...].reshape(256, 128)).astype(BF16)
    for j in (2, 1, 3):
        px_copy(x_at(j), x).start()
    o_bands[x] = o_own[...]

    spread_row = iota((128, 512), 0)
    spread_col = iota((128, 512), 1)
    spread = one_hot(
        jnp.logical_and(
            jnp.right_shift(spread_row, 4) == jnp.right_shift(spread_col, 6),
            jnp.bitwise_and(spread_row, 15) == jnp.bitwise_and(spread_col, 15),
        )
    )

    def wait_c(j):
        c_copy(grp_peer(j), grp_peer(j)).wait_recv()

    loop(1, N_GRP, wait_c)
    for k in range(4):
        up = dot(c_recv[:, k, :].astype(BF16), spread)
        for j in range(4):
            to_positions(coarse_rows, k * 4 + j, up[:, j * 128 : (j + 1) * 128])
    k_near[1, z] = dot_t(eye[:16], coarse_rows[...]).astype(BF16)
    for j in (4, 3, 5, 2, 6, 1, 7):
        kz_copy(z_at(j), z).start()

    for i in (0, 1):
        ring_wait(n_ring, i)
    spread_frames([1, 2])
    for i in (2, 3):
        ring_wait(n_ring, i)
    for i in (4, 5, 6, 7):
        ring_send(n_ring, i)
    spread_frames([3, 4])

    relay_frames([0])
    patches[...] = (
        signal_coef * coarse_rows[...].astype(F32) + noise_coef * noise_rows[...].astype(F32)
    ).astype(BF16)

    for j in (1, 3, 2):
        px_copy(x, x_at(j)).wait_recv()
    bands = [o_bands[j].astype(F32) for j in range(4)]
    for j in range(HD // 128):
        o_all[y, core, :, j * 128 : (j + 1) * 128] = jnp.concatenate(
            [band[j * 24 : (j + 1) * 24] for band in bands], axis=0
        ).astype(BF16)
    for i in range(4):
        ring_send(o_ring, i)
    od_copy(y, core).start()

    for i in (4, 5, 6, 7):
        ring_wait(n_ring, i)
    spread_frames([5, 6, 7])
    for j in (1, 7, 2, 6, 3, 5, 4):
        kz_copy(z, z_at(j)).wait_recv()
    kx_copy(0, 0).start()
    kx_copy(1, 0).start()
    relay_frames([1, 2, 3, 4])

    @pl.when(owner)
    def _():
        loop(1, N_Y, lambda j: y_copy(y_peer(j), y_peer(j)).wait_recv())
        cols = w_cols[...].reshape(D, 128)
        for c in (0, 1):
            both = dot(factors[c], cols)
            m_own[c] = (both[:ROWS] + both[ROWS:]).astype(BF16)

        def send_m(i):
            at_core, at_sp = m_target(i)

            @pl.when(jnp.logical_or(at_core != core, at_sp != s))
            def _():
                m_copy(i, block).start()

        loop(0, 2 * FH, send_m)
        m_all[block, pl.ds(0, ROWS), :] = m_own[core]

    relay_frames([5, 6, 7])

    kx_copy(0, 0).wait_recv()
    kx_copy(1, 0).wait_recv()
    kx_copy(0, 1).start()
    kx_copy(1, 1).start()

    natural = dot(perm[...], patches[...]).astype(BF16)
    for j in range(6):
        cols = slice(j * 256, (j + 1) * 256)
        hidden[:, cols] = dot(natural, padded_embed[:, cols]).astype(BF16)

    for i in range(4):
        ring_wait(o_ring, i)
    for i in (4, 5, 6, 7):
        ring_send(o_ring, i)
    for j in (1, -1, 2, -2):
        od_copy(y_at(j), core).start()

    def wait_m(b):
        @pl.when(not_here(b, half))
        def _():
            m_copy(core * 16 + place, b).wait_recv()

    def turn_m(blocks):
        for b in blocks:
            m_turned[b * 128 : (b + 1) * 128, :] = dot_t(eye, m_all[b])[:, :ROWS].astype(BF16)

    def frame_entries(coarse, noise):
        coarse = coarse.astype(F32)
        noise = noise.astype(F32)
        up = jnp.concatenate([coarse] * 4, axis=0)
        patch = (signal_coef * up + noise_coef * noise).astype(BF16)
        wide = patch.astype(F32)
        turned = dot(cov[...], patch)
        var = jnp.sum(wide * (turned[:64] + turned[64:128] + turned[128:]), axis=0, keepdims=True)
        wide = wide * lax.rsqrt(jnp.maximum(var, 0.0) + epsilon)
        return wide, jnp.concatenate([wide.astype(BF16), ones_row], axis=0)

    loop(0, 2 * PAIRS, wait_m)
    turn_m(range(2 * PAIRS))
    own = frame_entries(k_near[1, z], n_near[1, z])[1]
    for j in range(PAIRS):
        rows = slice(j * 128, (j + 1) * 128)
        q = dot(m_turned[rows, :], own).reshape(2, HEAD, TOKENS)
        level = jnp.sum(q * q, axis=1, keepdims=True) * (1.0 / HEAD) + epsilon
        q = (q * lax.rsqrt(level)).reshape(128, TOKENS)
        gain = jnp.concatenate([gains_turned[rows]] * 4, axis=1)
        query[rows, :] = q * gain

    ends = [clip_ref[0, 0]]
    for j in (1, 2, 3):
        ends.append(ends[-1] + clip_ref[0, j])
    first = jnp.int32(0)
    last = ends[0]
    for j in (1, 2, 3):
        inside = s >= ends[j - 1]
        first = jnp.where(inside, ends[j - 1], first)
        last = jnp.where(inside, ends[j], last)
    base = jnp.minimum(first, N_SP - WINDOW)

    near = jnp.minimum(jnp.maximum(s - base - WINDOW // 4, 0), WINDOW // 2)

    def frame_at(j):
        return base + jnp.bitwise_and(near + j, WINDOW - 1)

    def keys_of(j, buffer, far):
        t = frame_at(j)
        at_z = jnp.bitwise_and(t, 7)
        row = jnp.right_shift(t, 3) - x + 1
        near_row = jnp.minimum(jnp.maximum(row, 0), 2)
        coarse = k_near[near_row, at_z]
        noise = n_near[near_row, at_z]
        if far:
            inside = row == near_row
            coarse = jnp.where(inside, coarse, k_far[at_z])
            noise = jnp.where(inside, noise, n_far[at_z])
        wide, entries = frame_entries(coarse, noise)
        z_wide[j] = wide
        buffer[...] = dot(m_turned[HD : 2 * HD, :], entries)

    def score(j, buffer):
        for h in range(HEADS):
            k = buffer[h * HEAD : (h + 1) * HEAD, :]
            q = query[h * HEAD : (h + 1) * HEAD, :]
            dots[j, h] = jnp.sum((k * q).reshape(8, 8, TOKENS), axis=0)
            squares[j, h] = jnp.sum((k * k).reshape(8, 8, TOKENS), axis=0)

    def two_frames(far):
        def body(j):
            keys_of(2 * j + 1, keys_b, far)
            score(2 * j, keys_a)
            keys_of(after(2 * j + 2), keys_a, far)
            score(2 * j + 1, keys_b)

        return body

    def after(j):
        return jnp.where(j == WINDOW // 2, j - 1, jnp.minimum(j, WINDOW - 1))

    keys_of(0, keys_a, False)
    loop(0, WINDOW // 4, two_frames(False))
    kx_copy(0, 1).wait_recv()
    kx_copy(1, 1).wait_recv()
    for i in range(8):
        nr_copy(i).wait_recv()
    keys_of(WINDOW // 2, keys_a, True)
    loop(WINDOW // 4, WINDOW // 2, two_frames(True))
    for i in (4, 5, 6, 7):
        ring_wait(o_ring, i)
    for j in (3, -3, 4):
        od_copy(y_at(j), core).start()
    loop(2 * PAIRS, BLOCKS, wait_m)
    turn_m(range(2 * PAIRS, BLOCKS))
    def reduce_frame(j):
        scale = lax.rsqrt(jnp.sum(squares[j], axis=1) * (1.0 / HEAD) + epsilon)
        t = frame_at(j)
        valid = jnp.logical_and(t >= first, t < last)
        probs[j] = jnp.where(valid, jnp.sum(dots[j], axis=1) * scale, -1e30)

    loop(0, WINDOW, reduce_frame)
    expo = jnp.exp(probs[...] - jnp.max(probs[...], axis=0, keepdims=True))
    probs[...] = expo / jnp.sum(expo, axis=0, keepdims=True)

    def head(h):
        total = jnp.zeros((HEAD, TOKENS), F32)
        for j in range(WINDOW):
            total = total + probs[j, pl.ds(h, 1), :] * z_wide[j]
        blended[h, pl.ds(0, 64), :] = total.astype(BF16)

    loop(0, HEADS, head)
    for h in range(HEADS):
        rows = slice(h * HEAD, (h + 1) * HEAD)
        mixed_turned[rows, :] = dot(
            m_turned[2 * HD + h * HEAD : 2 * HD + (h + 1) * HEAD, :], blended[h]
        ).astype(BF16)

    loop(0, N_Y, lambda j: od_copy(j, 1 - core).wait_recv())
    for j in range(3):
        cols = slice(j * 256, (j + 1) * 256)
        mixed[:, cols] = dot_t(perm[...], mixed_turned[cols, :]).astype(BF16)
    for j in range(N_Y):
        cols = slice(j * 192, (j + 1) * 192)
        attn = dot_t(mixed[...], o_all[j].reshape(192, HD))
        out_ref[:, cols] = (hidden[:, cols].astype(F32) + attn).astype(BF16)

    loop(1, N_GRP, lambda j: c_copy(grp_peer(j), g).wait_send())

    def end_w(m):
        b = m // 2
        part = lax.rem(m, 2)

        @pl.when(not_here(b, part))
        def _():
            w_copy(b, part, plane).wait_send()

    loop(0, 2 * BLOCKS, end_w)
    for copy in d_copies():
        copy.wait_send()

    @pl.when(owner)
    def _():
        loop(1, N_Y, lambda j: y_copy(y_peer(j), y).wait_send())

        def end_m(i):
            at_core, at_sp = m_target(i)

            @pl.when(jnp.logical_or(at_core != core, at_sp != s))
            def _():
                m_copy(i, block).wait_send()

        loop(0, 2 * FH, end_m)

    for j in range(1, 8):
        pz_copy(z_at(j), z).wait_send()
    for j in (1, 2, 3):
        px_copy(x_at(j), x).wait_send()
    loop(0, N_Y, lambda j: od_copy(j, core).wait_send())
    for i in range(8):
        ring_end(n_ring, i)
        ring_end(o_ring, i)
        nx_copy(0, i).wait_send()
        nx_copy(1, i).wait_send()
        nr_copy(i).wait_send()
    for j in range(1, 8):
        kz_copy(z_at(j), z).wait_send()
    kx_copy(0, 0).wait_send()
    kx_copy(1, 0).wait_send()
    kx_copy(0, 1).wait_send()
    kx_copy(1, 1).wait_send()


def local(
    coarse_latent,
    renoise,
    clip_frames,
    patch_embed,
    mod_shift,
    mod_scale,
    qkv_weight,
    out_weight,
    q_gain,
    k_gain,
):
    dma = pltpu.SemaphoreType.DMA
    sems = [10, 16, 16, 36, 64, 8, 8, 2, 2, 32, 18, 8, 8, 4, 4, 8, 8, 8, 8] + [(2, 2)] * 2 + [8] * 6
    rings = [(2, 8)] * 2
    args = (
        coarse_latent.transpose(1, 2, 0, 3).reshape(N_GRP, FW * C),
        renoise,
        clip_frames,
        patch_embed,
        mod_shift,
        mod_scale,
        qkv_weight,
        out_weight,
        q_gain,
        k_gain,
    )
    inputs = [
        (pltpu.SMEM if a.dtype == jnp.int32 else pltpu.VMEM)(a.shape, a.dtype) for a in args
    ]
    return pl.pallas_call(
        kernel,
        out_shape=jax.ShapeDtypeStruct((TOKENS, D), BF16),
        in_specs=[pl.BlockSpec(memory_space=pltpu.HBM)] * len(args),
        out_specs=pl.BlockSpec(memory_space=pltpu.VMEM),
        scratch_shapes=inputs
        + [
            pltpu.VMEM((N_GRP, 8, 128), F32),
            pltpu.VMEM((N_GRP, 8, 128), F32),
            pltpu.VMEM((16, 3 * HD), BF16),
            pltpu.VMEM((32, 128), F32),
            pltpu.VMEM((32, 128), BF16),
            pltpu.VMEM((2 * N_SP, 16, 128), BF16),
            pltpu.VMEM((N_Y, 2 * PLANE_ROWS, 128), BF16),
            pltpu.VMEM((1, D), F32),
            pltpu.VMEM((1, D), F32),
            pltpu.VMEM((2, 2 * ROWS, D), BF16),
            pltpu.VMEM((2, ROWS, 128), BF16),
            pltpu.VMEM((BLOCKS, 128, 128), BF16),
            pltpu.VMEM((3 * HD, ROWS), BF16),
            pltpu.VMEM((TOKENS, 128), BF16),
            pltpu.VMEM((TOKENS, 128), BF16),
            pltpu.VMEM((TOKENS, 128), BF16),
            pltpu.VMEM((192, 64), BF16),
            pltpu.VMEM((3, 8, 64, TOKENS), BF16),
            pltpu.VMEM((8, 64, TOKENS), BF16),
            pltpu.VMEM((3, 8, 16, TOKENS), BF16),
            pltpu.VMEM((8, 16, TOKENS), BF16),
            pltpu.VMEM((WINDOW, HEAD, TOKENS), F32),
            pltpu.VMEM((8, 32, 128), BF16),
            pltpu.VMEM((144, 128), BF16),
            pltpu.VMEM((4, 144, 128), BF16),
            pltpu.VMEM((N_Y, 2, PLANE_ROWS, HD), BF16),
            pltpu.VMEM((TOKENS, TOKENS), BF16),
            pltpu.VMEM((HD, TOKENS), F32),
            pltpu.VMEM((HD, TOKENS), F32),
            pltpu.VMEM((HD, TOKENS), F32),
            pltpu.VMEM((WINDOW, HEADS, 8, TOKENS), F32),
            pltpu.VMEM((WINDOW, HEADS, 8, TOKENS), F32),
            pltpu.VMEM((WINDOW, HEADS, TOKENS), F32),
            pltpu.VMEM((HEADS, ROWS, TOKENS), BF16),
            pltpu.VMEM((HD, TOKENS), BF16),
            pltpu.VMEM((TOKENS, HD), BF16),
            pltpu.VMEM((128, D), BF16),
            pltpu.VMEM((TOKENS, D), BF16),
        ]
        + [dma(n if isinstance(n, tuple) else (n,)) for n in sems]
        + [dma(n) for n in rings],
        compiler_params=pltpu.CompilerParams(
            collective_id=0, has_side_effects=True, vmem_limit_bytes=63 * 1024 * 1024
        ),
    )(*args)


def solution(mesh):
    placed = (
        P(None, "sp", "grp", None),
        P(("grp", "sp"), None),
        P("grp", None),
        P(),
        P("grp", None),
        P("grp", None),
        P(("grp", "sp"), None),
        P(("grp", "sp"), None),
        P(),
        P(),
    )
    return jax.shard_map(
        local, mesh=mesh, in_specs=placed, out_specs=P(("grp", "sp"), None), check_vma=False
    )
```

time: 82.9 us -> 77.6 us (0.936)
  local copies, waits for them, and re-layouts: 8.47 us -> 2.65 us
    unnamed x20 -> x1, local copies, waits for them, and re-layouts: 8.47 us -> 2.65 us
    pallas_call x1, Pallas kernels: 74 us -> 74.8 us  [local(): pl.pallas_call(kernel, out_shape=jax.ShapeDtypeStruct((TOKENS, D), BF16),...]
where the time goes in v3:
time: 77.6 us; the launch traced here: 77.5 us
  Pallas kernels  74.8 us (96%)
  local copies, waits for them, and re-layouts  2.65 us (3%)
    pallas_call x1, Pallas kernels, local(): pl.pallas_call(kernel, out_shape=jax.ShapeDtypeStruct((TOKENS, D), BF16),...  74.8 us
    unnamed x1, local copies, waits for them, and re-layouts  2.65 us

profile of v3, /device:TPU:1, one launch (start us, length us, event | category | flops | bytes accessed | tf_op | source)
XLA Modules:
  0.0 77.5 jit_solution(9915761928265205015)
XLA Ops:
  0.0 74.8 %shard_map.100 = bf16[512,1536]{1,0:T(8,128)(2,1)} custom-call(bf16[16,512]{1,0:T(8,128)(2,1)} %bitcast.1, bf16[16,2048]{1,0:T(8,128)(2,1)} %noise_any.1, s32[1,4]{1,0:T(1,128)} %clip_any.1, bf16[64,1536]{1,0:T(8,128)(2,1)} %embed_any.1, f32[1,1536]{1,0:T(1,128)} %shift_any.1, f32[1,1536]{1,0:T(1,128)} %scale_any.1, bf16[3,2304]{1,0:T(4,128)(2,1)} %w_any.1, ...), custom_call_target="tpu_custom_call" | custom-call | tf_op jit(solution)/shard_map/pallas_call | solution.py:795
  74.8 2.7 %copy.12 = bf16[512,1536]{1,0:T(8,128)(2,1)} copy(bf16[512,1536]{1,0:T(8,128)(2,1)} %shard_map.100) | data formatting | bytes 3145728

commit v4 on v3

--- a/solution.py
+++ b/solution.py
@@ -106,7 +106,9 @@
     mixed,
     padded_embed,
     hidden,
+    result,
     in_s,
+    out_s,
     c_ss,
     c_rs,
     w_ss,
@@ -394,6 +396,9 @@
         def _():
             w_copy(b, part, plane).start()
 
+    for i in range(4):
+        ring_send(n_ring, i)
+    spread_frames([0])
     loop(0, 2 * BLOCKS, send_w)
 
     @pl.when(owner)
@@ -464,9 +469,15 @@
 
     loop(0, HEADS, pad_blended)
 
-    for i in range(4):
+
+    for i in (0, 1):
+        ring_wait(n_ring, i)
+    spread_frames([1, 2])
+    for i in (2, 3):
+        ring_wait(n_ring, i)
+    for i in (4, 5, 6, 7):
         ring_send(n_ring, i)
-    spread_frames([0])
+    spread_frames([3, 4])
 
     @pl.when(owner)
     def _():
@@ -518,16 +529,11 @@
     for j in (4, 3, 5, 2, 6, 1, 7):
         kz_copy(z_at(j), z).start()
 
-    for i in (0, 1):
+    relay_frames([0, 1, 2])
+    for i in (4, 5, 6, 7):
         ring_wait(n_ring, i)
-    spread_frames([1, 2])
-    for i in (2, 3):
-        ring_wait(n_ring, i)
-    for i in (4, 5, 6, 7):
-        ring_send(n_ring, i)
-    spread_frames([3, 4])
-
-    relay_frames([0])
+    spread_frames([5, 6, 7])
+    relay_frames([3, 4])
     patches[...] = (
         signal_coef * coarse_rows[...].astype(F32) + noise_coef * noise_rows[...].astype(F32)
     ).astype(BF16)
@@ -543,14 +549,10 @@
         ring_send(o_ring, i)
     od_copy(y, core).start()
 
-    for i in (4, 5, 6, 7):
-        ring_wait(n_ring, i)
-    spread_frames([5, 6, 7])
     for j in (1, 7, 2, 6, 3, 5, 4):
         kz_copy(z, z_at(j)).wait_recv()
     kx_copy(0, 0).start()
     kx_copy(1, 0).start()
-    relay_frames([1, 2, 3, 4])
 
     @pl.when(owner)
     def _():
@@ -636,7 +638,7 @@
     def frame_at(j):
         return base + jnp.bitwise_and(near + j, WINDOW - 1)
 
-    def keys_of(j, buffer, far):
+    def entries_at(j, far):
         t = frame_at(j)
         at_z = jnp.bitwise_and(t, 7)
         row = jnp.right_shift(t, 3) - x + 1
@@ -649,34 +651,47 @@
             noise = jnp.where(inside, noise, n_far[at_z])
         wide, entries = frame_entries(coarse, noise)
         z_wide[j] = wide
-        buffer[...] = dot(m_turned[HD : 2 * HD, :], entries)
-
-    def score(j, buffer):
-        for h in range(HEADS):
+        return entries
+
+    def keys_of(entries, buffer, part):
+        rows = slice(part * 256, (part + 1) * 256)
+        buffer[rows, :] = dot(m_turned[HD + part * 256 : HD + (part + 1) * 256, :], entries)
+
+    def score(j, buffer, part):
+        for h in range(part * 4, part * 4 + 4):
             k = buffer[h * HEAD : (h + 1) * HEAD, :]
             q = query[h * HEAD : (h + 1) * HEAD, :]
             dots[j, h] = jnp.sum((k * q).reshape(8, 8, TOKENS), axis=0)
             squares[j, h] = jnp.sum((k * k).reshape(8, 8, TOKENS), axis=0)
 
+    def step(j, buffer, following, other, far):
+        entries = entries_at(following, far)
+        for part in range(3):
+            keys_of(entries, other, part)
+            score(j, buffer, part)
+
+    def start(j, far):
+        entries = entries_at(j, far)
+        for part in range(3):
+            keys_of(entries, keys_a, part)
+
     def two_frames(far):
         def body(j):
-            keys_of(2 * j + 1, keys_b, far)
-            score(2 * j, keys_a)
-            keys_of(after(2 * j + 2), keys_a, far)
-            score(2 * j + 1, keys_b)
+            step(2 * j, keys_a, 2 * j + 1, keys_b, far)
+            step(2 * j + 1, keys_b, after(2 * j + 2), keys_a, far)
 
         return body
 
     def after(j):
         return jnp.where(j == WINDOW // 2, j - 1, jnp.minimum(j, WINDOW - 1))
 
-    keys_of(0, keys_a, False)
+    start(0, False)
     loop(0, WINDOW // 4, two_frames(False))
     kx_copy(0, 1).wait_recv()
     kx_copy(1, 1).wait_recv()
     for i in range(8):
         nr_copy(i).wait_recv()
-    keys_of(WINDOW // 2, keys_a, True)
+    start(WINDOW // 2, True)
     loop(WINDOW // 4, WINDOW // 2, two_frames(True))
     for i in (4, 5, 6, 7):
         ring_wait(o_ring, i)
@@ -711,11 +726,18 @@
     for j in range(3):
         cols = slice(j * 256, (j + 1) * 256)
         mixed[:, cols] = dot_t(perm[...], mixed_turned[cols, :]).astype(BF16)
-    for j in range(N_Y):
-        cols = slice(j * 192, (j + 1) * 192)
-        attn = dot_t(mixed[...], o_all[j].reshape(192, HD))
-        out_ref[:, cols] = (hidden[:, cols].astype(F32) + attn).astype(BF16)
-
+    stores = []
+    for j in range(4):
+        cols = slice(j * 384, (j + 1) * 384)
+        attn = dot_t(mixed[...], o_all[2 * j : 2 * j + 2].reshape(384, HD))
+        result[:, cols] = (hidden[:, cols].astype(F32) + attn).astype(BF16)
+        stores.append(
+            pltpu.make_async_copy(result.at[:, cols], out_ref.at[:, cols], out_s.at[j])
+        )
+        stores[-1].start()
+
+    for store in stores:
+        store.wait()
     loop(1, N_GRP, lambda j: c_copy(grp_peer(j), g).wait_send())
 
     def end_w(m):
@@ -775,7 +797,7 @@
     k_gain,
 ):
     dma = pltpu.SemaphoreType.DMA
-    sems = [10, 16, 16, 36, 64, 8, 8, 2, 2, 32, 18, 8, 8, 4, 4, 8, 8, 8, 8] + [(2, 2)] * 2 + [8] * 6
+    sems = [10, 4, 16, 16, 36, 64, 8, 8, 2, 2, 32, 18, 8, 8, 4, 4, 8, 8, 8, 8] + [(2, 2)] * 2 + [8] * 6
     rings = [(2, 8)] * 2
     args = (
         coarse_latent.transpose(1, 2, 0, 3).reshape(N_GRP, FW * C),
@@ -796,7 +818,7 @@
         kernel,
         out_shape=jax.ShapeDtypeStruct((TOKENS, D), BF16),
         in_specs=[pl.BlockSpec(memory_space=pltpu.HBM)] * len(args),
-        out_specs=pl.BlockSpec(memory_space=pltpu.VMEM),
+        out_specs=pl.BlockSpec(memory_space=pltpu.HBM),
         scratch_shapes=inputs
         + [
             pltpu.VMEM((N_GRP, 8, 128), F32),
@@ -837,6 +859,7 @@
             pltpu.VMEM((TOKENS, HD), BF16),
             pltpu.VMEM((128, D), BF16),
             pltpu.VMEM((TOKENS, D), BF16),
+            pltpu.VMEM((TOKENS, D), BF16),
         ]
         + [dma(n if isinstance(n, tuple) else (n,)) for n in sems]
         + [dma(n) for n in rings],

time: 77.6 us -> 75 us (0.966)
  Pallas kernels: 74.8 us -> 71.7 us
    pallas_call x1, Pallas kernels: 74.8 us -> 71.7 us  [local(): pl.pallas_call(kernel, out_shape=jax.ShapeDtypeStruct((TOKENS, D), BF16),...]
where the time goes in v4:
time: 75 us; the launch traced here: 74.3 us
  Pallas kernels  71.7 us (96%)
  local copies, waits for them, and re-layouts  2.65 us (4%)
    pallas_call x1, Pallas kernels, local(): pl.pallas_call(kernel, out_shape=jax.ShapeDtypeStruct((TOKENS, D), BF16),...  71.7 us
    unnamed x1, local copies, waits for them, and re-layouts  2.65 us

profile of v4, /device:TPU:1, one launch (start us, length us, event | category | flops | bytes accessed | tf_op | source)
XLA Modules:
  0.0 74.3 jit_solution(2778355092544200507)
XLA Ops:
  0.0 71.7 %shard_map.100 = bf16[512,1536]{1,0:T(8,128)(2,1)} custom-call(bf16[16,512]{1,0:T(8,128)(2,1)} %bitcast.1, bf16[16,2048]{1,0:T(8,128)(2,1)} %noise_any.1, s32[1,4]{1,0:T(1,128)} %clip_any.1, bf16[64,1536]{1,0:T(8,128)(2,1)} %embed_any.1, f32[1,1536]{1,0:T(1,128)} %shift_any.1, f32[1,1536]{1,0:T(1,128)} %scale_any.1, bf16[3,2304]{1,0:T(4,128)(2,1)} %w_any.1, ...), custom_call_target="tpu_custom_call" | custom-call | tf_op jit(solution)/shard_map/pallas_call | solution.py:817
  71.7 2.7 %copy.12 = bf16[512,1536]{1,0:T(8,128)(2,1)} copy(bf16[512,1536]{1,0:T(8,128)(2,1)} %shard_map.100) | data formatting | bytes 3145728

commit v5 on v4

--- a/solution.py
+++ b/solution.py
@@ -579,17 +579,17 @@
     kx_copy(0, 1).start()
     kx_copy(1, 1).start()
 
-    natural = dot(perm[...], patches[...]).astype(BF16)
-    for j in range(6):
-        cols = slice(j * 256, (j + 1) * 256)
-        hidden[:, cols] = dot(natural, padded_embed[:, cols]).astype(BF16)
-
     for i in range(4):
         ring_wait(o_ring, i)
     for i in (4, 5, 6, 7):
         ring_send(o_ring, i)
     for j in (1, -1, 2, -2):
         od_copy(y_at(j), core).start()
+
+    natural = dot(perm[...], patches[...]).astype(BF16)
+    for j in range(6):
+        cols = slice(j * 256, (j + 1) * 256)
+        hidden[:, cols] = dot(natural, padded_embed[:, cols]).astype(BF16)
 
     def wait_m(b):
         @pl.when(not_here(b, half))

time: 75 us -> 75.3 us (level)
  no operation moved by 1% of the time
where the time goes in v5:
time: 75.3 us; the launch traced here: 74.3 us
  Pallas kernels  71.7 us (95%)
  local copies, waits for them, and re-layouts  2.65 us (4%)
    pallas_call x1, Pallas kernels, local(): pl.pallas_call(kernel, out_shape=jax.ShapeDtypeStruct((TOKENS, D), BF16),...  71.7 us
    unnamed x1, local copies, waits for them, and re-layouts  2.65 us

profile of v5, /device:TPU:1, one launch (start us, length us, event | category | flops | bytes accessed | tf_op | source)
XLA Modules:
  0.0 74.3 jit_solution(5961391931783468328)
XLA Ops:
  0.0 71.7 %shard_map.100 = bf16[512,1536]{1,0:T(8,128)(2,1)} custom-call(bf16[16,512]{1,0:T(8,128)(2,1)} %bitcast.1, bf16[16,2048]{1,0:T(8,128)(2,1)} %noise_any.1, s32[1,4]{1,0:T(1,128)} %clip_any.1, bf16[64,1536]{1,0:T(8,128)(2,1)} %embed_any.1, f32[1,1536]{1,0:T(1,128)} %shift_any.1, f32[1,1536]{1,0:T(1,128)} %scale_any.1, bf16[3,2304]{1,0:T(4,128)(2,1)} %w_any.1, ...), custom_call_target="tpu_custom_call" | custom-call | tf_op jit(solution)/shard_map/pallas_call | solution.py:817
  71.7 2.7 %copy.12 = bf16[512,1536]{1,0:T(8,128)(2,1)} copy(bf16[512,1536]{1,0:T(8,128)(2,1)} %shard_map.100) | data formatting | bytes 3145728
